TPU v7x, 512 devices: a whole 4x4x16 slice. The times are simulated.
512 devices in a mesh: layer: 16 (over z), leaf: 32 (over y, x, core).
Axes of the slice: x: 4, y: 4, z: 16, core: 2. Of those that a mesh axis runs over, the one named last changes fastest.
Arguments:
- right_side: bfloat16 [16, 2, 32, 32768], P('layer', None, None, 'leaf'), may hold values from -6 to 6
- near_blocks: bfloat16 [16, 3, 2, 32768, 256], P('layer', None, None, 'leaf'), may hold values from -0.21875 to 0.21875
- right_bases: bfloat16 [16, 2, 2, 16, 32768], P('layer', None, None, None, 'leaf'), may hold values from -0.0625 to 0.0625
- left_bases: bfloat16 [16, 2, 2, 16, 32768], P('layer', None, None, None, 'leaf'), may hold values from -1 to 1
- coupling: bfloat16 [16, 32768], P('layer', 'leaf'), may hold values from 0.25 to 0.69921875
- ranks: int32 [16, 6], P('layer'), may hold values from 8 to 16
Outputs:
- swept: bfloat16 [16, 2, 32, 32768], P('layer', None, None, 'leaf')
Inputs may be any that keep to these rules, and one draw needn't show every extreme that they name: ranks[k, s] is the rank in use of layer k's far block that maps into cluster s at level 0 (s = 0, 1) or cluster s - 2 at level 1 (s = 2 to 5).
All inputs are finite; a program needn't handle non-finite values.
Results may differ from a plain program's by a relative error of at most 0.035.
Values may be sent and summed in bfloat16 or wider, within the bound.
No kernel may reach another device: no remote copies, remote signals or barrier semaphores. Data moves between devices by JAX's collectives and lax.ppermute only.
A program may use at most 64 MiB of HBM per device.

v0:
```python
import jax
import jax.numpy as jnp
from jax import lax
from jax.sharding import PartitionSpec as P


def extended(cells, sides, width):
    for axis, dim in sides:
        count = lax.axis_size(axis)
        ends = count - 1
        head = lax.slice_in_dim(cells, 0, width, axis=dim)
        tail = lax.slice_in_dim(cells, cells.shape[dim] - width, cells.shape[dim], axis=dim)
        cells = jnp.concatenate(
            [
                lax.ppermute(tail, axis, [(i, (i + 1) % count) for i in range(ends)]),
                cells,
                lax.ppermute(head, axis, [((i + 1) % count, i) for i in range(ends)]),
            ],
            axis=dim,
        )
    return cells


def sent_to_all(value, axis):
    copies = jnp.broadcast_to(value, (lax.axis_size(axis), *value.shape))
    return lax.all_to_all(copies, axis, split_axis=0, concat_axis=0, tiled=True)


def of_everyone(value, axis):
    return sent_to_all(value, axis).sum(axis=0)


def passed_along(value, axis, by):
    count = lax.axis_size(axis)
    pairs = [(i, i + by) for i in range(count) if 0 <= i + by < count]
    return lax.ppermute(value, axis, pairs)


def complex_rows(field, matrix):
    contract_dims = (((1,), (1,)), ((), ()))

    def single(first, second):
        return lax.dot_general(first, second, contract_dims, preferred_element_type=jnp.float32)

    real_part = single(field[0], matrix[0]) - single(field[1], matrix[1])
    imag_part = single(field[0], matrix[1]) + single(field[1], matrix[0])
    return jnp.stack([real_part, imag_part])


def complex_mul(coeff, basis):

    def single(first, second):
        return jnp.dot(first, second, preferred_element_type=jnp.float32)

    real_part = single(coeff[0], basis[0]) - single(coeff[1], basis[1])
    imag_part = single(coeff[0], basis[1]) + single(coeff[1], basis[0])
    return jnp.stack([real_part, imag_part])


def block_rows(field, blocks):
    form = "rlp,lqp->rlq"

    def single(first, second):
        return jnp.einsum(form, first, second, preferred_element_type=jnp.float32)

    real_part = single(field[0], blocks[0]) - single(field[1], blocks[1])
    imag_part = single(field[0], blocks[1]) + single(field[1], blocks[0])
    return jnp.stack([real_part, imag_part])


def body(right_side, near_blocks, right_bases, left_bases, coupling, ranks):
    leaf_count = lax.axis_size("leaf")
    layer_count = lax.axis_size("layer")
    layer_index = lax.axis_index("layer")
    leaf_index = lax.axis_index("leaf")
    source = right_side[0]
    cells = near_blocks.shape[-1]
    width_local = source.shape[2]
    leaves = width_local // cells
    blocks = near_blocks[0].reshape(3, 2, leaves, cells, cells)
    own_right = right_bases[0]
    own_left = left_bases[0]
    own_coupling = coupling[0]
    rank_row = ranks[0]
    rank_size = own_right.shape[2]
    slot_ids = jnp.arange(6)
    upper_cluster = leaf_index // (leaf_count // 2)
    lower_cluster = leaf_index // (leaf_count // 4)
    weight_upper = (slot_ids == upper_cluster).astype(jnp.float32)
    weight_lower = (slot_ids == 2 + lower_cluster).astype(jnp.float32)
    rank_upper = jnp.sum(jnp.where(slot_ids == upper_cluster, rank_row, 0))
    rank_lower = jnp.sum(jnp.where(slot_ids == 2 + lower_cluster, rank_row, 0))
    rank_ids = jnp.arange(rank_size)

    def slot_terms(field):
        first = complex_rows(field, own_right[0])
        second = complex_rows(field, own_right[1])
        return (
            weight_upper[:, None, None, None] * first[None]
            + weight_lower[:, None, None, None] * second[None]
        )

    def far_value(slot_totals):
        first = lax.dynamic_index_in_dim(
            slot_totals, jnp.bitwise_xor(upper_cluster, 1), 0, keepdims=False
        )
        second = lax.dynamic_index_in_dim(
            slot_totals, 2 + jnp.bitwise_xor(lower_cluster, 1), 0, keepdims=False
        )
        first = (first * (rank_ids < rank_upper).astype(jnp.float32)).astype(jnp.bfloat16)
        second = (second * (rank_ids < rank_lower).astype(jnp.float32)).astype(jnp.bfloat16)
        return complex_mul(first, own_left[0]) + complex_mul(second, own_left[1])

    def apply_local(field, lower_rim, upper_rim):
        slot_totals = of_everyone(slot_terms(field), "leaf")
        rows = field.shape[1]
        padded = jnp.concatenate([lower_rim, field, upper_rim], axis=2)
        own_part = field.reshape(2, rows, leaves, cells)
        lower_part = padded[:, :, :width_local].reshape(2, rows, leaves, cells)
        upper_part = padded[:, :, 2 * cells :].reshape(2, rows, leaves, cells)
        total = block_rows(own_part, blocks[0])
        total = total + block_rows(lower_part, blocks[1])
        total = total + block_rows(upper_part, blocks[2])
        return total.reshape(2, rows, width_local) + far_value(slot_totals)

    sides = extended(source, (("leaf", 2),), cells)
    source_lower = sides[:, :, :cells]
    source_upper = sides[:, :, -cells:]
    inner = apply_local(source, source_lower, source_upper)
    batch_count = 1
    row_count = source.shape[1] // batch_count
    inner_groups = inner.reshape(2, batch_count, row_count, width_local)

    def turn(turn_index, current):
        sent_group = jnp.clip(turn_index - 1 - layer_index, 0, batch_count - 1)
        outgoing = lax.dynamic_index_in_dim(current, sent_group, 1, keepdims=False)
        coupled = (own_coupling.astype(jnp.float32) * outgoing.astype(jnp.float32)).astype(
            jnp.bfloat16
        )
        received = passed_along(coupled, "layer", 1)
        rims = []
        for step_by, piece in (
            (leaf_count + 1, coupled[:, :, -cells:]),
            (leaf_count - 1, coupled[:, :, :cells]),
        ):
            rims.append(passed_along(piece, ("layer", "leaf"), step_by))
        lower_rim = jnp.where(leaf_index > 0, rims[0], jnp.zeros_like(rims[0]))
        upper_rim = jnp.where(leaf_index < leaf_count - 1, rims[1], jnp.zeros_like(rims[1]))
        update = apply_local(received, lower_rim, upper_rim)
        taken_group = turn_index - layer_index
        receiving = (taken_group >= 0) & (taken_group < batch_count) & (layer_index >= 1)
        taken_index = jnp.clip(taken_group, 0, batch_count - 1)
        previous = lax.dynamic_index_in_dim(inner_groups, taken_index, 1, keepdims=False)
        fresh = (previous - update).astype(jnp.bfloat16)
        written = lax.dynamic_update_index_in_dim(current, fresh, taken_index, 1)
        return jnp.where(receiving, written, current)

    forward = lax.fori_loop(
        1, layer_count + batch_count - 1, turn, inner_groups.astype(jnp.bfloat16)
    )
    return forward.reshape(2, source.shape[1], width_local)[None]


def solution(mesh):
    placed = (
        P("layer", None, None, "leaf"),
        P("layer", None, None, "leaf", None),
        P("layer", None, None, None, "leaf"),
        P("layer", None, None, None, "leaf"),
        P("layer", "leaf"),
        P("layer", None),
    )
    return jax.shard_map(
        body, mesh=mesh, in_specs=placed, out_specs=P("layer", None, None, "leaf"), check_vma=False
    )
```

profile of v0, /device:TPU:1, one launch (start us, length us, event | category | flops | bytes accessed | tf_op | source)
XLA Modules:
  0.0 1374.3 jit_solution(14017091131505175519)
XLA Ops:
  1.6 4.5 collective-permute-start.3
  6.1 6.2 collective-permute-start.4
  32.9 3.7 reshape.628
  46.6 4.4 all-to-all-start.1
  65.2 4.5 reduce.2
  77.9 1295.7 %while.17 = (s32[]{:T(128)}, bf16[2,1,32,1024]{3,2,1,0:T(8,128)(2,1)S(1)}, s32[]{:T(128)}, pred[]{:T(512)}, bf16[1024]{0:T(1024)(128)(2,1)S(1)}, /*index=5*/bf16...) while((s32[]{:T(128)}, ...), condition=%wide.region_5.6_spmd.clone.clone, body=%wide.region_3.5_spmd.clone.clone.sunk | while | flops 220189792 | bytes 33668208 | solution.py:158
  83.4 4.8 collective-permute-start.1
  88.3 3.7 collective-permute-start.2
  111.6 3.7 reshape.632
  115.3 9.6 all-to-all-start
  154.4 4.5 reduce.4
  167.3 4.2 collective-permute-start
  172.9 5.8 collective-permute-start.1
  201.1 3.7 reshape.632
  204.8 9.4 all-to-all-start
  243.6 4.5 reduce.4
  261.1 6.7 collective-permute-start.1
  294.2 9.4 all-to-all-start
  333.1 4.5 reduce.4
  350.6 6.0 collective-permute-start.1
  378.2 3.7 reshape.632
  381.9 8.4 all-to-all-start
  419.7 4.5 reduce.4
  437.2 6.0 collective-permute-start.1
  464.8 3.7 reshape.632
  468.5 8.4 all-to-all-start
  506.3 4.5 reduce.4
  519.2 4.1 collective-permute-start
  524.7 6.0 collective-permute-start.1
  552.3 3.7 reshape.632
  556.0 8.4 all-to-all-start
  593.8 4.5 reduce.4
  611.3 6.0 collective-permute-start.1
  638.9 3.7 reshape.632
  642.6 8.4 all-to-all-start
  680.4 4.5 reduce.4
  697.9 5.1 collective-permute-start.1
  724.6 3.7 reshape.632
  728.2 8.4 all-to-all-start
  766.1 4.5 reduce.4
  783.6 4.5 collective-permute-start.1
  809.6 3.7 reshape.632
  813.3 8.4 all-to-all-start
  851.1 4.5 reduce.4
  868.7 4.5 collective-permute-start.1
  894.7 3.7 reshape.632
  898.3 8.4 all-to-all-start
  936.2 4.5 reduce.4
  953.7 4.5 collective-permute-start.1
  983.4 8.4 all-to-all-start
  1021.2 4.5 reduce.4
  1038.8 4.5 collective-permute-start.1
  1064.8 3.7 reshape.632
  1068.5 8.4 all-to-all-start
  1106.3 4.5 reduce.4
  1123.8 4.5 collective-permute-start.1
  1153.5 8.4 all-to-all-start
  1191.4 4.5 reduce.4
  1208.9 4.5 collective-permute-start.1
  1238.6 8.4 all-to-all-start
  1276.4 4.5 reduce.4
  1293.9 4.5 collective-permute-start.1
  1323.6 8.4 all-to-all-start
  1361.5 4.5 reduce.4
  (1409 shorter events, 1023.1 us)
Async XLA Ops:
  0.0 23.8 %copy-start = (bf16[1,3,2,1024,256]{4,3,2,1,0:T(8,128)(2,1)S(1)}, bf16[1,3,2,1024,256]{4,3,2,1,0:T(8,128)(2,1)}, u32[]{:S(2)}) copy-start(bf16[1,3,2,1024,256]{4,3,2,1,0:T(8,128)(2,1)} %param.9) | copy-start | bytes 9437188
  1.6 37.6 %collective-permute-start.3 = (bf16[2,32,256]{2,1,0:T(8,128)(2,1)}, bf16[2,32,256]{2,1,0:T(8,128)(2,1)}, u32[]{:S(2)}, u32[]{:S(2)}) collective-permute-start(bf16[2,32,256]{2,1,0:T(8,128)(2,1)} %get-tuple-element.541), channel_id=1, source_target_pairs={{0,1},{1,2},{2,3},{3,4},{4,5},{5,6},{6,7},{7,8},{8,9},{9,10},{10,1... | collective-permute-start | bytes 98312 | tf_op jit(solution)/shard_map/ppermute | solution.py:15
  6.1 33.1 %collective-permute-start.4 = (bf16[2,32,256]{2,1,0:T(8,128)(2,1)}, bf16[2,32,256]{2,1,0:T(8,128)(2,1)}, u32[]{:S(2)}, u32[]{:S(2)}) collective-permute-start(bf16[2,32,256]{2,1,0:T(8,128)(2,1)} %get-tuple-element.542), channel_id=1, source_target_pairs={{1,0},{2,1},{3,2},{4,3},{5,4},{6,5},{7,6},{8,7},{9,8},{10,9},{11,1... | collective-permute-start | bytes 98312 | tf_op jit(solution)/shard_map/ppermute | solution.py:17
  46.6 18.0 %all-to-all-start.1 = ((f32[32,1,6144]{2,1,0:T(1,128)}), f32[32,1,6144]{2,1,0:T(1,128)}, u32[]{:S(2)}, u32[]{:S(2)}) async-start(f32[32,1,6144]{2,1,0:T(1,128)} %reshape.628), calls=%async_computation.1 | async-start | bytes 1572864 | tf_op jit(solution)/shard_map/all_to_all | solution.py:26
  78.6 16.8 %collective-permute-start = (bf16[2,32,1024]{2,1,0:T(8,128)(2,1)}, bf16[2,32,1024]{2,1,0:T(8,128)(2,1)S(1)}, u32[]{:S(2)}, u32[]{:S(2)}) collective-permute-start(bf16[2,32,1024]{2,1,0:T(8,128)(2,1)} %fusion.364), channel_id=1, source_target_pairs={{0,32},{32,64},{64,96},{96,128},{128,160},{160,192},{192,224},{224... | collective-permute-start | bytes 393224 | tf_op jit(solution)/shard_map/while/body/eval_jaxpr/ppermute | solution.py:36
  83.4 10.5 collective-permute-start.1
  88.3 6.4 collective-permute-start.2
  115.3 38.5 %all-to-all-start = ((f32[32,1,6144]{2,1,0:T(1,128)}), f32[32,1,6144]{2,1,0:T(1,128)}, u32[]{:S(2)}, u32[]{:S(2)}) async-start(f32[32,1,6144]{2,1,0:T(1,128)} %reshape.632), calls=%async_computation | async-start | bytes 1572864 | tf_op jit(solution)/shard_map/while/body/eval_jaxpr/all_to_all | solution.py:26
  167.3 17.6 %collective-permute-start = (bf16[2,32,1024]{2,1,0:T(8,128)(2,1)}, bf16[2,32,1024]{2,1,0:T(8,128)(2,1)S(1)}, u32[]{:S(2)}, u32[]{:S(2)}) collective-permute-start(bf16[2,32,1024]{2,1,0:T(8,128)(2,1)} %fusion.364), channel_id=1, source_target_pairs={{0,32},{32,64},{64,96},{96,128},{128,160},{160,192},{192,224},{224... | collective-permute-start | bytes 393224 | tf_op jit(solution)/shard_map/while/body/eval_jaxpr/ppermute | solution.py:36
  172.9 10.5 collective-permute-start.1
  178.7 5.5 collective-permute-start.2
  204.8 38.3 %all-to-all-start = ((f32[32,1,6144]{2,1,0:T(1,128)}), f32[32,1,6144]{2,1,0:T(1,128)}, u32[]{:S(2)}, u32[]{:S(2)}) async-start(f32[32,1,6144]{2,1,0:T(1,128)} %reshape.632), calls=%async_computation | async-start | bytes 1572864 | tf_op jit(solution)/shard_map/while/body/eval_jaxpr/all_to_all | solution.py:26
  256.5 17.9 %collective-permute-start = (bf16[2,32,1024]{2,1,0:T(8,128)(2,1)}, bf16[2,32,1024]{2,1,0:T(8,128)(2,1)S(1)}, u32[]{:S(2)}, u32[]{:S(2)}) collective-permute-start(bf16[2,32,1024]{2,1,0:T(8,128)(2,1)} %fusion.364), channel_id=1, source_target_pairs={{0,32},{32,64},{64,96},{96,128},{128,160},{160,192},{192,224},{224... | collective-permute-start | bytes 393224 | tf_op jit(solution)/shard_map/while/body/eval_jaxpr/ppermute | solution.py:36
  261.1 11.7 collective-permute-start.1
  267.9 5.7 collective-permute-start.2
  294.2 38.3 %all-to-all-start = ((f32[32,1,6144]{2,1,0:T(1,128)}), f32[32,1,6144]{2,1,0:T(1,128)}, u32[]{:S(2)}, u32[]{:S(2)}) async-start(f32[32,1,6144]{2,1,0:T(1,128)} %reshape.632), calls=%async_computation | async-start | bytes 1572864 | tf_op jit(solution)/shard_map/while/body/eval_jaxpr/all_to_all | solution.py:26
  345.9 16.1 %collective-permute-start = (bf16[2,32,1024]{2,1,0:T(8,128)(2,1)}, bf16[2,32,1024]{2,1,0:T(8,128)(2,1)S(1)}, u32[]{:S(2)}, u32[]{:S(2)}) collective-permute-start(bf16[2,32,1024]{2,1,0:T(8,128)(2,1)} %fusion.364), channel_id=1, source_target_pairs={{0,32},{32,64},{64,96},{96,128},{128,160},{160,192},{192,224},{224... | collective-permute-start | bytes 393224 | tf_op jit(solution)/shard_map/while/body/eval_jaxpr/ppermute | solution.py:36
  350.6 9.8 collective-permute-start.1
  356.7 4.6 collective-permute-start.2
  381.9 37.3 %all-to-all-start = ((f32[32,1,6144]{2,1,0:T(1,128)}), f32[32,1,6144]{2,1,0:T(1,128)}, u32[]{:S(2)}, u32[]{:S(2)}) async-start(f32[32,1,6144]{2,1,0:T(1,128)} %reshape.632), calls=%async_computation | async-start | bytes 1572864 | tf_op jit(solution)/shard_map/while/body/eval_jaxpr/all_to_all | solution.py:26
  432.6 16.0 %collective-permute-start = (bf16[2,32,1024]{2,1,0:T(8,128)(2,1)}, bf16[2,32,1024]{2,1,0:T(8,128)(2,1)S(1)}, u32[]{:S(2)}, u32[]{:S(2)}) collective-permute-start(bf16[2,32,1024]{2,1,0:T(8,128)(2,1)} %fusion.364), channel_id=1, source_target_pairs={{0,32},{32,64},{64,96},{96,128},{128,160},{160,192},{192,224},{224... | collective-permute-start | bytes 393224 | tf_op jit(solution)/shard_map/while/body/eval_jaxpr/ppermute | solution.py:36
  437.2 9.8 collective-permute-start.1
  443.3 4.6 collective-permute-start.2
  468.5 37.3 %all-to-all-start = ((f32[32,1,6144]{2,1,0:T(1,128)}), f32[32,1,6144]{2,1,0:T(1,128)}, u32[]{:S(2)}, u32[]{:S(2)}) async-start(f32[32,1,6144]{2,1,0:T(1,128)} %reshape.632), calls=%async_computation | async-start | bytes 1572864 | tf_op jit(solution)/shard_map/while/body/eval_jaxpr/all_to_all | solution.py:26
  519.2 16.9 %collective-permute-start = (bf16[2,32,1024]{2,1,0:T(8,128)(2,1)}, bf16[2,32,1024]{2,1,0:T(8,128)(2,1)S(1)}, u32[]{:S(2)}, u32[]{:S(2)}) collective-permute-start(bf16[2,32,1024]{2,1,0:T(8,128)(2,1)} %fusion.364), channel_id=1, source_target_pairs={{0,32},{32,64},{64,96},{96,128},{128,160},{160,192},{192,224},{224... | collective-permute-start | bytes 393224 | tf_op jit(solution)/shard_map/while/body/eval_jaxpr/ppermute | solution.py:36
  524.7 9.8 collective-permute-start.1
  530.8 4.6 collective-permute-start.2
  556.0 37.3 %all-to-all-start = ((f32[32,1,6144]{2,1,0:T(1,128)}), f32[32,1,6144]{2,1,0:T(1,128)}, u32[]{:S(2)}, u32[]{:S(2)}) async-start(f32[32,1,6144]{2,1,0:T(1,128)} %reshape.632), calls=%async_computation | async-start | bytes 1572864 | tf_op jit(solution)/shard_map/while/body/eval_jaxpr/all_to_all | solution.py:26
  606.7 16.0 %collective-permute-start = (bf16[2,32,1024]{2,1,0:T(8,128)(2,1)}, bf16[2,32,1024]{2,1,0:T(8,128)(2,1)S(1)}, u32[]{:S(2)}, u32[]{:S(2)}) collective-permute-start(bf16[2,32,1024]{2,1,0:T(8,128)(2,1)} %fusion.364), channel_id=1, source_target_pairs={{0,32},{32,64},{64,96},{96,128},{128,160},{160,192},{192,224},{224... | collective-permute-start | bytes 393224 | tf_op jit(solution)/shard_map/while/body/eval_jaxpr/ppermute | solution.py:36
  611.3 9.8 collective-permute-start.1
  617.4 4.6 collective-permute-start.2
  642.6 37.3 %all-to-all-start = ((f32[32,1,6144]{2,1,0:T(1,128)}), f32[32,1,6144]{2,1,0:T(1,128)}, u32[]{:S(2)}, u32[]{:S(2)}) async-start(f32[32,1,6144]{2,1,0:T(1,128)} %reshape.632), calls=%async_computation | async-start | bytes 1572864 | tf_op jit(solution)/shard_map/while/body/eval_jaxpr/all_to_all | solution.py:26
  693.3 15.1 %collective-permute-start = (bf16[2,32,1024]{2,1,0:T(8,128)(2,1)}, bf16[2,32,1024]{2,1,0:T(8,128)(2,1)S(1)}, u32[]{:S(2)}, u32[]{:S(2)}) collective-permute-start(bf16[2,32,1024]{2,1,0:T(8,128)(2,1)} %fusion.364), channel_id=1, source_target_pairs={{0,32},{32,64},{64,96},{96,128},{128,160},{160,192},{192,224},{224... | collective-permute-start | bytes 393224 | tf_op jit(solution)/shard_map/while/body/eval_jaxpr/ppermute | solution.py:36
  697.9 8.9 collective-permute-start.1
  703.0 4.6 collective-permute-start.2
  728.2 37.3 %all-to-all-start = ((f32[32,1,6144]{2,1,0:T(1,128)}), f32[32,1,6144]{2,1,0:T(1,128)}, u32[]{:S(2)}, u32[]{:S(2)}) async-start(f32[32,1,6144]{2,1,0:T(1,128)} %reshape.632), calls=%async_computation | async-start | bytes 1572864 | tf_op jit(solution)/shard_map/while/body/eval_jaxpr/all_to_all | solution.py:26
  779.0 14.5 %collective-permute-start = (bf16[2,32,1024]{2,1,0:T(8,128)(2,1)}, bf16[2,32,1024]{2,1,0:T(8,128)(2,1)S(1)}, u32[]{:S(2)}, u32[]{:S(2)}) collective-permute-start(bf16[2,32,1024]{2,1,0:T(8,128)(2,1)} %fusion.364), channel_id=1, source_target_pairs={{0,32},{32,64},{64,96},{96,128},{128,160},{160,192},{192,224},{224... | collective-permute-start | bytes 393224 | tf_op jit(solution)/shard_map/while/body/eval_jaxpr/ppermute | solution.py:36
  783.6 8.3 collective-permute-start.1
  788.1 4.6 collective-permute-start.2
  813.3 37.3 %all-to-all-start = ((f32[32,1,6144]{2,1,0:T(1,128)}), f32[32,1,6144]{2,1,0:T(1,128)}, u32[]{:S(2)}, u32[]{:S(2)}) async-start(f32[32,1,6144]{2,1,0:T(1,128)} %reshape.632), calls=%async_computation | async-start | bytes 1572864 | tf_op jit(solution)/shard_map/while/body/eval_jaxpr/all_to_all | solution.py:26
  864.0 14.5 %collective-permute-start = (bf16[2,32,1024]{2,1,0:T(8,128)(2,1)}, bf16[2,32,1024]{2,1,0:T(8,128)(2,1)S(1)}, u32[]{:S(2)}, u32[]{:S(2)}) collective-permute-start(bf16[2,32,1024]{2,1,0:T(8,128)(2,1)} %fusion.364), channel_id=1, source_target_pairs={{0,32},{32,64},{64,96},{96,128},{128,160},{160,192},{192,224},{224... | collective-permute-start | bytes 393224 | tf_op jit(solution)/shard_map/while/body/eval_jaxpr/ppermute | solution.py:36
  868.7 8.3 collective-permute-start.1
  873.1 4.6 collective-permute-start.2
  898.3 37.3 %all-to-all-start = ((f32[32,1,6144]{2,1,0:T(1,128)}), f32[32,1,6144]{2,1,0:T(1,128)}, u32[]{:S(2)}, u32[]{:S(2)}) async-start(f32[32,1,6144]{2,1,0:T(1,128)} %reshape.632), calls=%async_computation | async-start | bytes 1572864 | tf_op jit(solution)/shard_map/while/body/eval_jaxpr/all_to_all | solution.py:26
  949.1 14.5 %collective-permute-start = (bf16[2,32,1024]{2,1,0:T(8,128)(2,1)}, bf16[2,32,1024]{2,1,0:T(8,128)(2,1)S(1)}, u32[]{:S(2)}, u32[]{:S(2)}) collective-permute-start(bf16[2,32,1024]{2,1,0:T(8,128)(2,1)} %fusion.364), channel_id=1, source_target_pairs={{0,32},{32,64},{64,96},{96,128},{128,160},{160,192},{192,224},{224... | collective-permute-start | bytes 393224 | tf_op jit(solution)/shard_map/while/body/eval_jaxpr/ppermute | solution.py:36
  953.7 8.3 collective-permute-start.1
  958.2 4.6 collective-permute-start.2
  983.4 37.3 %all-to-all-start = ((f32[32,1,6144]{2,1,0:T(1,128)}), f32[32,1,6144]{2,1,0:T(1,128)}, u32[]{:S(2)}, u32[]{:S(2)}) async-start(f32[32,1,6144]{2,1,0:T(1,128)} %reshape.632), calls=%async_computation | async-start | bytes 1572864 | tf_op jit(solution)/shard_map/while/body/eval_jaxpr/all_to_all | solution.py:26
  1034.1 14.5 %collective-permute-start = (bf16[2,32,1024]{2,1,0:T(8,128)(2,1)}, bf16[2,32,1024]{2,1,0:T(8,128)(2,1)S(1)}, u32[]{:S(2)}, u32[]{:S(2)}) collective-permute-start(bf16[2,32,1024]{2,1,0:T(8,128)(2,1)} %fusion.364), channel_id=1, source_target_pairs={{0,32},{32,64},{64,96},{96,128},{128,160},{160,192},{192,224},{224... | collective-permute-start | bytes 393224 | tf_op jit(solution)/shard_map/while/body/eval_jaxpr/ppermute | solution.py:36
  1038.8 8.3 collective-permute-start.1
  1043.2 4.6 collective-permute-start.2
  1068.5 37.3 %all-to-all-start = ((f32[32,1,6144]{2,1,0:T(1,128)}), f32[32,1,6144]{2,1,0:T(1,128)}, u32[]{:S(2)}, u32[]{:S(2)}) async-start(f32[32,1,6144]{2,1,0:T(1,128)} %reshape.632), calls=%async_computation | async-start | bytes 1572864 | tf_op jit(solution)/shard_map/while/body/eval_jaxpr/all_to_all | solution.py:26
  1119.2 14.5 %collective-permute-start = (bf16[2,32,1024]{2,1,0:T(8,128)(2,1)}, bf16[2,32,1024]{2,1,0:T(8,128)(2,1)S(1)}, u32[]{:S(2)}, u32[]{:S(2)}) collective-permute-start(bf16[2,32,1024]{2,1,0:T(8,128)(2,1)} %fusion.364), channel_id=1, source_target_pairs={{0,32},{32,64},{64,96},{96,128},{128,160},{160,192},{192,224},{224... | collective-permute-start | bytes 393224 | tf_op jit(solution)/shard_map/while/body/eval_jaxpr/ppermute | solution.py:36
  1123.8 8.3 collective-permute-start.1
  1128.3 4.6 collective-permute-start.2
  1153.5 37.3 %all-to-all-start = ((f32[32,1,6144]{2,1,0:T(1,128)}), f32[32,1,6144]{2,1,0:T(1,128)}, u32[]{:S(2)}, u32[]{:S(2)}) async-start(f32[32,1,6144]{2,1,0:T(1,128)} %reshape.632), calls=%async_computation | async-start | bytes 1572864 | tf_op jit(solution)/shard_map/while/body/eval_jaxpr/all_to_all | solution.py:26
  1204.2 14.5 %collective-permute-start = (bf16[2,32,1024]{2,1,0:T(8,128)(2,1)}, bf16[2,32,1024]{2,1,0:T(8,128)(2,1)S(1)}, u32[]{:S(2)}, u32[]{:S(2)}) collective-permute-start(bf16[2,32,1024]{2,1,0:T(8,128)(2,1)} %fusion.364), channel_id=1, source_target_pairs={{0,32},{32,64},{64,96},{96,128},{128,160},{160,192},{192,224},{224... | collective-permute-start | bytes 393224 | tf_op jit(solution)/shard_map/while/body/eval_jaxpr/ppermute | solution.py:36
  1208.9 8.3 collective-permute-start.1
  1213.4 4.6 collective-permute-start.2
  1238.6 37.3 %all-to-all-start = ((f32[32,1,6144]{2,1,0:T(1,128)}), f32[32,1,6144]{2,1,0:T(1,128)}, u32[]{:S(2)}, u32[]{:S(2)}) async-start(f32[32,1,6144]{2,1,0:T(1,128)} %reshape.632), calls=%async_computation | async-start | bytes 1572864 | tf_op jit(solution)/shard_map/while/body/eval_jaxpr/all_to_all | solution.py:26
  1289.3 14.5 %collective-permute-start = (bf16[2,32,1024]{2,1,0:T(8,128)(2,1)}, bf16[2,32,1024]{2,1,0:T(8,128)(2,1)S(1)}, u32[]{:S(2)}, u32[]{:S(2)}) collective-permute-start(bf16[2,32,1024]{2,1,0:T(8,128)(2,1)} %fusion.364), channel_id=1, source_target_pairs={{0,32},{32,64},{64,96},{96,128},{128,160},{160,192},{192,224},{224... | collective-permute-start | bytes 393224 | tf_op jit(solution)/shard_map/while/body/eval_jaxpr/ppermute | solution.py:36
  1293.9 8.3 collective-permute-start.1
  1298.4 4.6 collective-permute-start.2
  1323.6 37.3 %all-to-all-start = ((f32[32,1,6144]{2,1,0:T(1,128)}), f32[32,1,6144]{2,1,0:T(1,128)}, u32[]{:S(2)}, u32[]{:S(2)}) async-start(f32[32,1,6144]{2,1,0:T(1,128)} %reshape.632), calls=%async_computation | async-start | bytes 1572864 | tf_op jit(solution)/shard_map/while/body/eval_jaxpr/all_to_all | solution.py:26
  (160 other events, 961.8 us)
where the time goes:
time: 1400 us; the launch traced here: 1370 us
  local copies, waits for them, and re-layouts  501 us (36%)
  matrix products  369 us (26%)
  starting transfers between devices  304 us (22%)
  other arithmetic  192 us (14%)
    dot_general x192, matrix products, single(): return jnp.einsum(form, first, second, preferred_element_type=jnp.float32)  221 us
    ppermute x45, starting transfers between devices, passed_along(): return lax.ppermute(value, axis, pairs)  160 us
    while x345, local copies, waits for them, and re-layouts  138 us
    another operation x96, local copies, waits for them, and re-layouts, block_rows(): return jnp.stack([real_part, imag_part])  136 us
    all_to_all x16, starting transfers between devices, sent_to_all(): return lax.all_to_all(copies, axis, split_axis=0, concat_axis=0, tiled=True)  133 us
    dot_general x128, matrix products, single(): lax.dot_general(first, second, contract_dims, preferred_element_type=jnp....  125 us
    all_to_all x16, other arithmetic, sent_to_all(): return lax.all_to_all(copies, axis, split_axis=0, concat_axis=0, tiled=True)  72.1 us
    squeeze x96, local copies, waits for them, and re-layouts, block_rows(): real_part = single(field[0], blocks[0]) - single(field[1], blocks[1])  66.9 us
  transfers between devices with their start and end apart: 63, of which 1 were waited for; matrix products, arithmetic and copies ran while one was open for 39% of the time, Pallas kernels for 0%

commit v1 on v0

v1 whole, which is shorter than its diff:
```python
import functools

import jax
import jax.numpy as jnp
from jax import lax
from jax.experimental import pallas as pl
from jax.experimental.pallas import tpu as pltpu
from jax.sharding import PartitionSpec as P

CELLS = 256
ROWS = 64
HALF = 32
LANES = 128
BF16 = jnp.bfloat16
F32 = jnp.float32
GRANT = 24 * 1024 * 1024


def row_dot(first, second):
    return lax.dot_general(first, second, (((1,), (1,)), ((), ())), preferred_element_type=F32)


def mat_dot(first, second):
    return jnp.dot(first, second, preferred_element_type=F32)


def turned(field):
    return jnp.concatenate([-field[HALF:], field[:HALF]], axis=0)


def coefficients(field, right):
    return row_dot(field[:HALF], right) + row_dot(field[HALF:], turned(right))


def packed(coeff):
    return jnp.concatenate([coeff[:16], coeff[16:]], axis=1)


def unpacked(dense):
    return jnp.concatenate([dense[:, :ROWS], dense[:, ROWS:]], axis=0)


def by_quarter(sums):
    return jnp.concatenate([unpacked(sums[q]) for q in range(4)], axis=1)


def seen(quarter, viewer):
    level = (lax.broadcasted_iota(jnp.int32, (ROWS, 1), 0) // 16) % 2
    far_half = jnp.where(viewer // 2 == quarter // 2, 0.0, 1.0).astype(F32)
    sibling = jnp.where(jnp.bitwise_xor(viewer, 1) == quarter, 1.0, 0.0).astype(F32)
    return jnp.where(level == 0, far_half, sibling)


def weights_of(basis):
    real, imag = basis[:HALF], basis[HALF:]
    return jnp.concatenate([real, -imag], axis=0), jnp.concatenate([imag, real], axis=0)


def far_rows(coeff, weights_ref):
    width = weights_ref.shape[1] // 2
    both = mat_dot(coeff, weights_ref[...])
    return jnp.concatenate([both[:, :width], both[:, width:]], axis=0)


def near_leaf(leaf, leaves, own, lower, upper, blocks_ref, total=None):
    rows = slice(leaf * CELLS, (leaf + 1) * CELLS)
    below = own[leaf - 1] if leaf else lower
    above = own[leaf + 1] if leaf + 1 < leaves else upper
    for side, part in ((0, own[leaf]), (1, below), (2, above)):
        if part is None:
            continue
        term = row_dot(part, blocks_ref[side, 0, rows, :])
        term = term + row_dot(turned(part), blocks_ref[side, 1, rows, :])
        total = term if total is None else total + term
    return total


def first_kernel(field, lower, upper, basis, basis_low, basis_up, blocks, right, near, ext, ext_low, ext_up, sums):
    width = field.shape[1]
    leaves = width // CELLS
    own_x = [field[:, j * CELLS : (j + 1) * CELLS] for j in range(leaves)]
    own_b = [basis[:, j * CELLS : (j + 1) * CELLS] for j in range(leaves)]
    for j in range(leaves):
        cols = slice(j * CELLS, (j + 1) * CELLS)
        near[:, cols] = near_leaf(j, leaves, own_x, lower[...], upper[...], blocks)
        ext[:, cols] = near_leaf(j, leaves, own_b, None, None, blocks)
    rows = slice(0, CELLS)
    edge = row_dot(basis_low[...], blocks[1, 0, rows, :])
    ext_low[...] = edge + row_dot(turned(basis_low[...]), blocks[1, 1, rows, :])
    rows = slice((leaves - 1) * CELLS, leaves * CELLS)
    edge = row_dot(basis_up[...], blocks[2, 0, rows, :])
    ext_up[...] = edge + row_dot(turned(basis_up[...]), blocks[2, 1, rows, :])
    sums[:16] = packed(coefficients(field[...], right[...])).astype(BF16)
    sums[16:] = packed(coefficients(basis[...], right[...])).astype(BF16)


def emit_field(value, coupling, right_next, carried, out, out_low, out_up, out_sums):
    width = value.shape[1]
    sent = (coupling * value).astype(BF16)
    out[:, :width] = sent
    out[:HALF, width:] = carried[:, :LANES]
    out[HALF:, width:] = carried[:, LANES:]
    out_low[...] = sent[:, :CELLS]
    out_up[...] = sent[:, width - CELLS :]
    out_sums[...] = packed(coefficients(sent, right_next)).astype(BF16)


def second_kernel(
    place, all_sums, near, left, ext, ext_low, ext_up, coupling, right_next,
    base, left_w, ext_w, carry_w, out, out_low, out_up, out_sums,
):
    width = near.shape[1]
    mine, low_view, up_view = place[1], place[2], place[3]
    left_r, left_i = weights_of(left[...].astype(F32))
    ext_r, ext_i = weights_of(ext[...])
    low_r, low_i = weights_of(ext_low[...])
    up_r, up_i = weights_of(ext_up[...])
    last = width - CELLS
    for q in range(4):
        rows = slice(q * ROWS, (q + 1) * ROWS)
        own_mask, low_mask, up_mask = seen(q, mine), seen(q, low_view), seen(q, up_view)
        for at, left_p, ext_p, low_p, up_p in ((0, left_r, ext_r, low_r, up_r), (width, left_i, ext_i, low_i, up_i)):
            left_w[rows, at : at + width] = (left_p * own_mask).astype(BF16)
            ext_m = ext_p * own_mask
            ext_w[rows, at : at + CELLS] = (ext_m[:, :CELLS] + low_p * low_mask).astype(BF16)
            ext_w[rows, at + CELLS : at + last] = ext_m[:, CELLS:last].astype(BF16)
            ext_w[rows, at + last : at + width] = (ext_m[:, last:] + up_p * up_mask).astype(BF16)
    sums = jnp.sum(all_sums[...].astype(F32).reshape(4, -1, HALF, LANES), axis=1)
    coeff = by_quarter(sums[:, :16]).astype(BF16)
    columns = []
    for q in range(4):
        real = unpacked(sums[q, 16:])
        imag = jnp.concatenate([-real[:, HALF:], real[:, :HALF]], axis=1)
        block = jnp.concatenate([real, imag], axis=0)
        columns.append(jnp.concatenate([block * seen(s, q) for s in range(4)], axis=0))
    carry_w[...] = jnp.concatenate(columns, axis=1).astype(BF16)
    value = near[...] + far_rows(coeff, left_w)
    base[...] = value
    emit_field(
        value, coupling[...], right_next[...], jnp.zeros((HALF, 2 * LANES), BF16), out, out_low, out_up, out_sums
    )


def turn_kernel(
    place, turn, field, lower, upper, all_sums, blocks, base, ext_w, carry_w, coupling, right_next, old_value, old_coeff,
    value_out, coeff_out, out, out_low, out_up, out_sums,
):
    @pl.when(place[0] == turn[0])
    def _():
        width = base.shape[1]
        leaves = width // CELLS
        sums = jnp.sum(all_sums[...].astype(F32).reshape(4, -1, 16, LANES), axis=1)
        carried = jnp.concatenate([field[:HALF, width:], field[HALF:, width:]], axis=1)
        coeff = (by_quarter(sums) - carried.astype(F32)).astype(BF16)
        coeff_out[...] = coeff
        own = [field[:, j * CELLS : (j + 1) * CELLS] for j in range(leaves)]
        near = [near_leaf(j, leaves, own, lower[...], upper[...], blocks) for j in range(leaves)]
        value = base[...] - jnp.concatenate(near, axis=1) + far_rows(coeff, ext_w)
        value_out[...] = value
        onward = mat_dot(coeff, carry_w[...]).astype(BF16)
        emit_field(value, coupling[...], right_next[...], onward, out, out_low, out_up, out_sums)

    @pl.when(place[0] != turn[0])
    def _():
        value_out[...] = old_value[...]
        coeff_out[...] = old_coeff[...]


def last_kernel(place, layers, received, field, all_sums, value, left_w, out):
    width = value.shape[1]
    sums = jnp.sum(all_sums[...].astype(F32).reshape(4, -1, 16, LANES), axis=1)
    coeff = received[...]
    carried = jnp.concatenate([field[:HALF, width:], field[HALF:, width:]], axis=1).astype(F32)
    final = (by_quarter(sums) - carried).astype(BF16)
    coeff = jnp.where(place[0] == layers[0] - 1, final.astype(F32), coeff.astype(F32)).astype(BF16)
    out[...] = (value[...] - far_rows(coeff, left_w)).astype(BF16)


def vmem(count):
    return [pl.BlockSpec(memory_space=pltpu.VMEM)] * count


def smem(count):
    return [pl.BlockSpec(memory_space=pltpu.SMEM)] * count


def shape(dims, dtype):
    return jax.ShapeDtypeStruct(dims, dtype)


def body(right_side, near_blocks, right_bases, left_bases, coupling, ranks):
    layer_count = lax.axis_size("layer")
    leaf_count = lax.axis_size("leaf")
    layer = lax.axis_index("layer")
    leaf = lax.axis_index("leaf")
    width = right_side.shape[3]
    field = right_side[0].reshape(ROWS, width)
    blocks = near_blocks[0]
    own_coupling = coupling[0].astype(F32).reshape(1, width)
    right = right_bases[0].transpose(1, 0, 2, 3).reshape(ROWS, width)
    per_quarter = leaf_count // 4
    mine = leaf // per_quarter
    place = jnp.stack([layer, mine, (leaf + per_quarter - 1) // per_quarter - 1, (leaf + 1) // per_quarter])
    place = place.astype(jnp.int32)
    rank_row = ranks[0]
    slots = jnp.arange(6)
    limits = jnp.stack(
        [jnp.sum(jnp.where(slots == mine // 2, rank_row, 0)), jnp.sum(jnp.where(slots == 2 + mine, rank_row, 0))]
    )
    keep = jnp.arange(16)[None, :] < limits[:, None]
    left = jnp.where(keep[:, None, :, None], left_bases[0], jnp.zeros((), BF16))
    left = left.transpose(1, 0, 2, 3).reshape(ROWS, width)
    basis = (left.astype(F32) * own_coupling).astype(BF16)

    def beside(value, by):
        return lax.ppermute(value, "leaf", [(i, i + by) for i in range(leaf_count) if 0 <= i + by < leaf_count])

    def back(value):
        return lax.ppermute(value, "layer", [(i + 1, i) for i in range(layer_count - 1)])

    def ahead(value, turn, by, hop=1):
        pairs = [
            (k * leaf_count + i, (k + hop) * leaf_count + i + by)
            for k in range(layer_count - hop)
            if (k - turn) % 3 == 0
            for i in range(leaf_count)
            if 0 <= i + by < leaf_count
        ]
        return lax.ppermute(value, ("layer", "leaf"), pairs)

    def all_ahead(value, by):
        pairs = [
            (k * leaf_count + i, (k + 1) * leaf_count + i + by)
            for k in range(layer_count - 1)
            for i in range(leaf_count)
            if 0 <= i + by < leaf_count
        ]
        return lax.ppermute(value, ("layer", "leaf"), pairs)

    def to_all(value):
        copies = jnp.broadcast_to(value, (leaf_count, *value.shape))
        return lax.all_to_all(copies, "leaf", split_axis=0, concat_axis=0, tiled=True)

    def to_all_of(turn, value):
        return lax.cond(
            layer == turn, to_all, lambda v: jnp.zeros((leaf_count, *v.shape), v.dtype), value
        )

    params = pltpu.CompilerParams(vmem_limit_bytes=GRANT)
    lower = beside(field[:, width - CELLS :], 1)
    upper = beside(field[:, :CELLS], -1)
    basis_in = all_ahead(basis, 0)
    basis_low = all_ahead(basis[:, width - CELLS :], 1)
    basis_up = all_ahead(basis[:, :CELLS], -1)
    right_next = back(right)
    near, ext, ext_low, ext_up, sums = pl.pallas_call(
        first_kernel,
        out_shape=[
            shape((ROWS, width), F32), shape((ROWS, width), F32), shape((ROWS, CELLS), F32),
            shape((ROWS, CELLS), F32), shape((HALF, LANES), BF16),
        ],
        in_specs=vmem(8), out_specs=vmem(5), compiler_params=params, name="first",
    )(field, lower, upper, basis_in, basis_low, basis_up, blocks, right)
    base, left_w, ext_w, carry_w, sent, sent_low, sent_up, sums = pl.pallas_call(
        second_kernel,
        out_shape=[
            shape((ROWS, width), F32), shape((256, 2 * width), BF16), shape((256, 2 * width), BF16),
            shape((256, 256), BF16), shape((ROWS, width + LANES), BF16), shape((ROWS, CELLS), BF16),
            shape((ROWS, CELLS), BF16), shape((16, LANES), BF16),
        ],
        in_specs=smem(1) + vmem(8), out_specs=vmem(8), compiler_params=params, name="second",
    )(place, to_all(sums), near, left, ext, ext_low, ext_up, own_coupling, right_next)

    value = base
    coeff = jnp.zeros((HALF, 256), BF16)
    no_sums = jnp.zeros((leaf_count, 16, LANES), BF16)
    early = None
    turn_call = pl.pallas_call(
        turn_kernel,
        out_shape=[
            shape((ROWS, width), F32), shape((HALF, 256), BF16), shape((ROWS, width + LANES), BF16),
            shape((ROWS, CELLS), BF16), shape((ROWS, CELLS), BF16), shape((16, LANES), BF16),
        ],
        in_specs=smem(2) + vmem(12), out_specs=vmem(6), input_output_aliases={12: 0, 13: 1},
        compiler_params=params, name="turn",
    )
    for turn in range(1, layer_count):
        got = ahead(sent, turn - 1, 0)
        got_low = ahead(sent_up, turn - 1, 1)
        got_up = ahead(sent_low, turn - 1, -1)
        last_turn = turn == layer_count - 1
        next_early = ahead(sums, turn - 1, 0, 1 if last_turn else 2)
        summed = no_sums if early is None else to_all_of(turn, early)
        early = next_early
        value, coeff, sent, sent_low, sent_up, sums = turn_call(
            place, jnp.full((1,), turn, jnp.int32), got, got_low, got_up, summed, blocks, base, ext_w, carry_w,
            own_coupling, right_next, value, coeff,
        )
    summed = to_all_of(layer_count - 1, early)
    out = pl.pallas_call(
        last_kernel,
        out_shape=shape((ROWS, width), BF16),
        in_specs=smem(2) + vmem(5), out_specs=vmem(1)[0], compiler_params=params, name="last",
    )(place, jnp.full((1,), layer_count, jnp.int32), back(coeff), sent, summed, value, left_w)
    return out.reshape(2, HALF, width)[None]


def solution(mesh):
    placed = (
        P("layer", None, None, "leaf"),
        P("layer", None, None, "leaf", None),
        P("layer", None, None, None, "leaf"),
        P("layer", None, None, None, "leaf"),
        P("layer", "leaf"),
        P("layer", None),
    )
    return jax.shard_map(
        body, mesh=mesh, in_specs=placed, out_specs=P("layer", None, None, "leaf"), check_vma=False
    )
```

time: 1400 us -> 399 us (0.28)
  the two profiles are of different devices: /device:TPU:1 before, /device:TPU:481 now
where the time goes in v1:
time: 399 us; the launch traced here: 395 us
  waiting for transfers between devices  141 us (35%)
  starting transfers between devices  100 us (25%)
  local copies, waits for them, and re-layouts  89 us (22%)
  Pallas kernels  34.2 us (9%)
  blocking collectives  24.4 us (6%)
  other arithmetic  4.65 us (1%)
    ppermute x60, waiting for transfers between devices, ahead(): return lax.ppermute(value, ('layer', 'leaf'), pairs)  136 us
    unnamed x191, local copies, waits for them, and re-layouts  77.1 us
    ppermute x60, starting transfers between devices, ahead(): return lax.ppermute(value, ('layer', 'leaf'), pairs)  74.7 us
    pallas_call x15, Pallas kernels, body(): turn_call(place, jnp.full((1,), turn, jnp.int32), got, got_low, got_up, s...  28.1 us
    all_to_all x2, blocking collectives, to_all(): lax.all_to_all(copies, 'leaf', split_axis=0, concat_axis=0, tiled=True)  24.4 us
    all_to_all x1, starting transfers between devices, to_all(): lax.all_to_all(copies, 'leaf', split_axis=0, concat_axis=0, tiled=True)  8.81 us
    another operation x14, local copies, waits for them, and re-layouts  8.77 us
  transfers between devices with their start and end apart: 68, of which 13 were waited for; matrix products, arithmetic and copies ran while one was open for 3% of the time, Pallas kernels for 0%

profile of v1, /device:TPU:481, one launch (start us, length us, event | category | flops | bytes accessed | tf_op | source)
XLA Modules:
  0.0 394.7 jit_solution(12971776859285146553)
XLA Ops:
  0.0 1.4 fusion.1
  1.4 1.4 pad_add_fusion.1
  4.6 1.3 collective-permute-start.2
  5.9 1.3 collective-permute-start.3
  7.2 1.3 collective-permute-start.4
  9.3 3.7 collective-permute-start
  13.0 1.9 collective-permute-start.1
  15.9 2.4 collective-permute-done.1.upper
  18.2 1.9 copy-done
  21.0 2.1 first.1
  26.6 8.8 %all-to-all-start.15 = ((bf16[32,32,128]{2,1,0:T(8,128)(2,1)}), bf16[32,32,128]{2,1,0:T(8,128)(2,1)}, u32[]{:S(2)}, u32[]{:S(2)}) async-start(bf16[32,32,128]{2,1,0:T(8,128)(2,1)} %broadcast_in_dim.74), calls=%async_computation.15 | async-start | bytes 524288 | tf_op jit(solution)/shard_map/all_to_all | solution.py:242
  35.4 6.1 %collective-permute-start.5 = (bf16[64,1024]{1,0:T(8,128)(2,1)S(1)}, bf16[64,1024]{1,0:T(8,128)(2,1)S(1)}, u32[]{:S(2)}, u32[]{:S(2)}) collective-permute-start(bf16[64,1024]{1,0:T(8,128)(2,1)S(1)} %bitcast.44), channel_id=1, source_target_pairs={{32,0},{64,32},{96,64},{128,96},{160,128},{192,160},{224,192},{256... | collective-permute-start | bytes 393224 | tf_op jit(solution)/shard_map/ppermute | solution.py:219
  41.6 2.5 collective-permute-done.5.right_next
  48.0 2.4 second.1
  54.8 1.3 turn.15
  57.0 1.3 collective-permute-start.9
  67.1 1.8 turn.16
  70.2 1.3 collective-permute-start.14
  71.5 1.3 collective-permute-start.15
  72.8 1.3 collective-permute-start.16
  74.1 17.5 %collective-permute-done.16 = bf16[16,128]{1,0:T(8,128)(2,1)} collective-permute-done((bf16[16,128]{1,0:T(8,128)(2,1)}, bf16[16,128]{1,0:T(8,128)(2,1)}, u32[]{:S(2)}, u32[]{:S(2)}) %collective-permute-start.16) | collective-permute-done | bytes 4128 | tf_op jit(solution)/shard_map/ppermute | solution.py:229
  97.3 1.8 turn.17
  99.1 1.3 collective-permute-start.17
  109.2 1.8 turn.18
  111.0 1.3 collective-permute-start.21
  121.1 1.8 turn.19
  124.2 1.3 collective-permute-start.26
  125.5 1.3 collective-permute-start.27
  126.8 1.3 collective-permute-start.28
  128.1 9.7 %collective-permute-done.28 = bf16[16,128]{1,0:T(8,128)(2,1)} collective-permute-done((bf16[16,128]{1,0:T(8,128)(2,1)}, bf16[16,128]{1,0:T(8,128)(2,1)}, u32[]{:S(2)}, u32[]{:S(2)}) %collective-permute-start.28) | collective-permute-done | bytes 4128 | tf_op jit(solution)/shard_map/ppermute | solution.py:229
  143.5 2.0 turn.20
  145.5 1.3 collective-permute-start.29
  155.6 1.8 turn.21
  157.4 1.3 collective-permute-start.33
  167.5 1.8 turn.22
  170.6 1.3 collective-permute-start.38
  171.9 1.3 collective-permute-start.39
  173.2 1.3 collective-permute-start.40
  174.5 9.9 %collective-permute-done.40 = bf16[16,128]{1,0:T(8,128)(2,1)} collective-permute-done((bf16[16,128]{1,0:T(8,128)(2,1)}, bf16[16,128]{1,0:T(8,128)(2,1)}, u32[]{:S(2)}, u32[]{:S(2)}) %collective-permute-start.40) | collective-permute-done | bytes 4128 | tf_op jit(solution)/shard_map/ppermute | solution.py:229
  190.6 1.8 turn.23
  192.4 1.3 collective-permute-start.41
  202.5 1.8 turn.24
  204.3 1.3 collective-permute-start.45
  214.4 1.8 turn.25
  217.5 1.3 collective-permute-start.50
  218.8 1.3 collective-permute-start.51
  220.1 1.3 collective-permute-start.52
  221.4 8.8 %collective-permute-done.52 = bf16[16,128]{1,0:T(8,128)(2,1)} collective-permute-done((bf16[16,128]{1,0:T(8,128)(2,1)}, bf16[16,128]{1,0:T(8,128)(2,1)}, u32[]{:S(2)}, u32[]{:S(2)}) %collective-permute-start.52) | collective-permute-done | bytes 4128 | tf_op jit(solution)/shard_map/ppermute | solution.py:229
  236.5 1.8 turn.26
  238.3 1.3 collective-permute-start.53
  248.4 2.0 turn.27
  250.4 1.3 collective-permute-start.57
  260.5 1.8 turn.28
  264.2 1.3 collective-permute-start.62
  265.5 1.3 collective-permute-start.63
  268.1 83.4 %collective-permute-done.64 = bf16[16,128]{1,0:T(8,128)(2,1)} collective-permute-done((bf16[16,128]{1,0:T(8,128)(2,1)}, bf16[16,128]{1,0:T(8,128)(2,1)}, u32[]{:S(2)}, u32[]{:S(2)}) %collective-permute-start.64) | collective-permute-done | bytes 4128 | tf_op jit(solution)/shard_map/ppermute | solution.py:229
  351.4 12.7 %conditional.28 = (bf16[32,16,128]{2,1,0:T(8,128)(2,1)}) conditional(s32[]{:T(128)} %convert_element_type.69, () %tuple.108, bf16[16,128]{1,0:T(8,128)(2,1)} %collective-permute-done.64), branch_computations={%region_28.29_spmd, %region_29.30_spmd} | conditional | bytes 397320 | solution.py:245
  352.1 12.0 %all_to_all.78 = bf16[32,16,128]{2,1,0:T(8,128)(2,1)} all-to-all(bf16[32,16,128]{2,1,0:T(8,128)(2,1)S(1)} %broadcast_in_dim.64), channel_id=1, replica_groups=mesh['layer'=16,'leaf'=32] {'leaf'}, dimensions={0} | all-to-all | bytes 262144 | tf_op jit(solution)/shard_map/cond/branch_1_fun/all_to_all | solution.py:242
  368.5 3.2 turn.29
  373.6 1.3 collective-permute-start.66
  374.9 3.1 collective-permute-done.66
  378.0 12.4 %conditional.29 = (bf16[32,16,128]{2,1,0:T(8,128)(2,1)S(1)}) conditional(s32[]{:T(128)} %convert_element_type.69, () %tuple.109, bf16[16,128]{1,0:T(8,128)(2,1)S(1)} %collective-permute-done.66), branch_computations={%region_30.31_spmd, %region_31.32_spmd} | conditional | bytes 397320 | solution.py:245
  378.0 12.4 %all_to_all.79 = bf16[32,16,128]{2,1,0:T(8,128)(2,1)S(1)} all-to-all(bf16[32,16,128]{2,1,0:T(8,128)(2,1)S(1)} %broadcast_in_dim.65), channel_id=1, replica_groups=mesh['layer'=16,'leaf'=32] {'leaf'}, dimensions={0} | all-to-all | bytes 262144 | tf_op jit(solution)/shard_map/cond/branch_1_fun/all_to_all | solution.py:242
  393.2 1.6 last.1
  (327 shorter events, 146.6 us)
Async XLA Ops:
  4.6 13.6 %collective-permute-start.2 = (bf16[64,1024]{1,0:T(8,128)(2,1)S(1)}, bf16[64,1024]{1,0:T(8,128)(2,1)S(1)}, u32[]{:S(2)}, u32[]{:S(2)}) collective-permute-start(bf16[64,1024]{1,0:T(8,128)(2,1)S(1)} %multiply_convert_fusion), channel_id=1, source_target_pairs={{0,32},{1,33},{2,34},{3,35},{4,36},{5,37},{6,38},{7,39},{8,40},{9,... | collective-permute-start | bytes 393224 | tf_op jit(solution)/shard_map/ppermute | solution.py:238
  5.9 9.9 %collective-permute-start.3 = (bf16[64,256]{1,0:T(8,128)(2,1)S(1)}, bf16[64,256]{1,0:T(8,128)(2,1)S(1)}, u32[]{:S(2)}, u32[]{:S(2)}) collective-permute-start(bf16[64,256]{1,0:T(8,128)(2,1)S(1)} %get-tuple-element.268), channel_id=1, source_target_pairs={{0,33},{1,34},{2,35},{3,36},{4,37},{5,38},{6,39},{7,40},{8,41},{9,... | collective-permute-start | bytes 98312 | tf_op jit(solution)/shard_map/ppermute | solution.py:238
  7.2 8.6 %collective-permute-start.4 = (bf16[64,256]{1,0:T(8,128)(2,1)S(1)}, bf16[64,256]{1,0:T(8,128)(2,1)S(1)}, u32[]{:S(2)}, u32[]{:S(2)}) collective-permute-start(bf16[64,256]{1,0:T(8,128)(2,1)S(1)} %get-tuple-element.267), channel_id=1, source_target_pairs={{1,32},{2,33},{3,34},{4,35},{5,36},{6,37},{7,38},{8,39},{9,40},{10... | collective-permute-start | bytes 98312 | tf_op jit(solution)/shard_map/ppermute | solution.py:238
  9.3 6.5 %collective-permute-start = (bf16[64,256]{1,0:T(8,128)(2,1)S(1)}, bf16[64,256]{1,0:T(8,128)(2,1)S(1)}, u32[]{:S(2)}, u32[]{:S(2)}) collective-permute-start(bf16[64,256]{1,0:T(8,128)(2,1)S(1)} %get-tuple-element.270), channel_id=1, source_target_pairs={{0,1},{1,2},{2,3},{3,4},{4,5},{5,6},{6,7},{7,8},{8,9},{9,10},{10,1... | collective-permute-start | bytes 98312 | tf_op jit(solution)/shard_map/ppermute | solution.py:216
  13.0 5.2 %collective-permute-start.1 = (bf16[64,256]{1,0:T(8,128)(2,1)S(1)}, bf16[64,256]{1,0:T(8,128)(2,1)S(1)}, u32[]{:S(2)}, u32[]{:S(2)}) collective-permute-start(bf16[64,256]{1,0:T(8,128)(2,1)S(1)} %get-tuple-element.269), channel_id=1, source_target_pairs={{1,0},{2,1},{3,2},{4,3},{5,4},{6,5},{7,6},{8,7},{9,8},{10,9},{11,1... | collective-permute-start | bytes 98312 | tf_op jit(solution)/shard_map/ppermute | solution.py:216
  26.6 17.8 %all-to-all-start.15 = ((bf16[32,32,128]{2,1,0:T(8,128)(2,1)}), bf16[32,32,128]{2,1,0:T(8,128)(2,1)}, u32[]{:S(2)}, u32[]{:S(2)}) async-start(bf16[32,32,128]{2,1,0:T(8,128)(2,1)} %broadcast_in_dim.74), calls=%async_computation.15 | async-start | bytes 524288 | tf_op jit(solution)/shard_map/all_to_all | solution.py:242
  35.4 8.6 %collective-permute-start.5 = (bf16[64,1024]{1,0:T(8,128)(2,1)S(1)}, bf16[64,1024]{1,0:T(8,128)(2,1)S(1)}, u32[]{:S(2)}, u32[]{:S(2)}) collective-permute-start(bf16[64,1024]{1,0:T(8,128)(2,1)S(1)} %bitcast.44), channel_id=1, source_target_pairs={{32,0},{64,32},{96,64},{128,96},{160,128},{192,160},{224,192},{256... | collective-permute-start | bytes 393224 | tf_op jit(solution)/shard_map/ppermute | solution.py:219
  51.4 2.1 collective-permute-start.6
  52.0 1.4 collective-permute-start.7
  57.0 5.8 %collective-permute-start.9 = (bf16[64,1152]{1,0:T(8,128)(2,1)}, bf16[64,1152]{1,0:T(8,128)(2,1)}, u32[]{:S(2)}, u32[]{:S(2)}) collective-permute-start(bf16[64,1152]{1,0:T(8,128)(2,1)} %get-tuple-element.176), channel_id=1, source_target_pairs={{32,64},{33,65},{34,66},{35,67},{36,68},{37,69},{38,70},{39,71},{4... | collective-permute-start | bytes 442376 | tf_op jit(solution)/shard_map/ppermute | solution.py:229
  58.4 4.4 %collective-permute-start.10 = (bf16[64,256]{1,0:T(8,128)(2,1)}, bf16[64,256]{1,0:T(8,128)(2,1)}, u32[]{:S(2)}, u32[]{:S(2)}) collective-permute-start(bf16[64,256]{1,0:T(8,128)(2,1)} %get-tuple-element.177), channel_id=1, source_target_pairs={{32,65},{33,66},{34,67},{35,68},{36,69},{37,70},{38,71},{39,72},{4... | collective-permute-start | bytes 98312 | tf_op jit(solution)/shard_map/ppermute | solution.py:229
  59.6 3.2 collective-permute-start.11
  60.9 1.2 collective-permute-start.12
  68.9 24.0 %collective-permute-start.13 = (bf16[64,1152]{1,0:T(8,128)(2,1)}, bf16[64,1152]{1,0:T(8,128)(2,1)}, u32[]{:S(2)}, u32[]{:S(2)}) collective-permute-start(bf16[64,1152]{1,0:T(8,128)(2,1)} %get-tuple-element.182), channel_id=1, source_target_pairs={{64,96},{65,97},{66,98},{67,99},{68,100},{69,101},{70,102},{71,103... | collective-permute-start | bytes 442376 | tf_op jit(solution)/shard_map/ppermute | solution.py:229
  70.2 22.1 %collective-permute-start.14 = (bf16[64,256]{1,0:T(8,128)(2,1)}, bf16[64,256]{1,0:T(8,128)(2,1)}, u32[]{:S(2)}, u32[]{:S(2)}) collective-permute-start(bf16[64,256]{1,0:T(8,128)(2,1)} %get-tuple-element.183), channel_id=1, source_target_pairs={{64,97},{65,98},{66,99},{67,100},{68,101},{69,102},{70,103},{71,10... | collective-permute-start | bytes 98312 | tf_op jit(solution)/shard_map/ppermute | solution.py:229
  71.5 21.4 %collective-permute-start.15 = (bf16[64,256]{1,0:T(8,128)(2,1)}, bf16[64,256]{1,0:T(8,128)(2,1)}, u32[]{:S(2)}, u32[]{:S(2)}) collective-permute-start(bf16[64,256]{1,0:T(8,128)(2,1)} %get-tuple-element.184), channel_id=1, source_target_pairs={{65,96},{66,97},{67,98},{68,99},{69,100},{70,101},{71,102},{72,103... | collective-permute-start | bytes 98312 | tf_op jit(solution)/shard_map/ppermute | solution.py:229
  72.8 18.8 %collective-permute-start.16 = (bf16[16,128]{1,0:T(8,128)(2,1)}, bf16[16,128]{1,0:T(8,128)(2,1)}, u32[]{:S(2)}, u32[]{:S(2)}) collective-permute-start(bf16[16,128]{1,0:T(8,128)(2,1)} %get-tuple-element.185), channel_id=1, source_target_pairs={{32,96},{33,97},{34,98},{35,99},{36,100},{37,101},{38,102},{39,103... | collective-permute-start | bytes 12296 | tf_op jit(solution)/shard_map/ppermute | solution.py:229
  99.1 5.8 %collective-permute-start.17 = (bf16[64,1152]{1,0:T(8,128)(2,1)}, bf16[64,1152]{1,0:T(8,128)(2,1)}, u32[]{:S(2)}, u32[]{:S(2)}) collective-permute-start(bf16[64,1152]{1,0:T(8,128)(2,1)} %get-tuple-element.188), channel_id=1, source_target_pairs={{0,32},{1,33},{2,34},{3,35},{4,36},{5,37},{6,38},{7,39},{8,40},{9,... | collective-permute-start | bytes 442376 | tf_op jit(solution)/shard_map/ppermute | solution.py:229
  100.4 4.4 %collective-permute-start.18 = (bf16[64,256]{1,0:T(8,128)(2,1)}, bf16[64,256]{1,0:T(8,128)(2,1)}, u32[]{:S(2)}, u32[]{:S(2)}) collective-permute-start(bf16[64,256]{1,0:T(8,128)(2,1)} %get-tuple-element.189), channel_id=1, source_target_pairs={{0,33},{1,34},{2,35},{3,36},{4,37},{5,38},{6,39},{7,40},{8,41},{9,... | collective-permute-start | bytes 98312 | tf_op jit(solution)/shard_map/ppermute | solution.py:229
  101.6 3.2 collective-permute-start.19
  102.9 1.2 collective-permute-start.20
  111.0 5.8 %collective-permute-start.21 = (bf16[64,1152]{1,0:T(8,128)(2,1)}, bf16[64,1152]{1,0:T(8,128)(2,1)}, u32[]{:S(2)}, u32[]{:S(2)}) collective-permute-start(bf16[64,1152]{1,0:T(8,128)(2,1)} %get-tuple-element.194), channel_id=1, source_target_pairs={{32,64},{33,65},{34,66},{35,67},{36,68},{37,69},{38,70},{39,71},{4... | collective-permute-start | bytes 442376 | tf_op jit(solution)/shard_map/ppermute | solution.py:229
  112.3 4.4 %collective-permute-start.22 = (bf16[64,256]{1,0:T(8,128)(2,1)}, bf16[64,256]{1,0:T(8,128)(2,1)}, u32[]{:S(2)}, u32[]{:S(2)}) collective-permute-start(bf16[64,256]{1,0:T(8,128)(2,1)} %get-tuple-element.195), channel_id=1, source_target_pairs={{32,65},{33,66},{34,67},{35,68},{36,69},{37,70},{38,71},{39,72},{4... | collective-permute-start | bytes 98312 | tf_op jit(solution)/shard_map/ppermute | solution.py:229
  113.5 3.2 collective-permute-start.23
  122.9 16.3 %collective-permute-start.25 = (bf16[64,1152]{1,0:T(8,128)(2,1)}, bf16[64,1152]{1,0:T(8,128)(2,1)}, u32[]{:S(2)}, u32[]{:S(2)}) collective-permute-start(bf16[64,1152]{1,0:T(8,128)(2,1)} %get-tuple-element.200), channel_id=1, source_target_pairs={{64,96},{65,97},{66,98},{67,99},{68,100},{69,101},{70,102},{71,103... | collective-permute-start | bytes 442376 | tf_op jit(solution)/shard_map/ppermute | solution.py:229
  124.2 14.3 %collective-permute-start.26 = (bf16[64,256]{1,0:T(8,128)(2,1)}, bf16[64,256]{1,0:T(8,128)(2,1)}, u32[]{:S(2)}, u32[]{:S(2)}) collective-permute-start(bf16[64,256]{1,0:T(8,128)(2,1)} %get-tuple-element.201), channel_id=1, source_target_pairs={{64,97},{65,98},{66,99},{67,100},{68,101},{69,102},{70,103},{71,10... | collective-permute-start | bytes 98312 | tf_op jit(solution)/shard_map/ppermute | solution.py:229
  125.5 13.7 %collective-permute-start.27 = (bf16[64,256]{1,0:T(8,128)(2,1)}, bf16[64,256]{1,0:T(8,128)(2,1)}, u32[]{:S(2)}, u32[]{:S(2)}) collective-permute-start(bf16[64,256]{1,0:T(8,128)(2,1)} %get-tuple-element.202), channel_id=1, source_target_pairs={{65,96},{66,97},{67,98},{68,99},{69,100},{70,101},{71,102},{72,103... | collective-permute-start | bytes 98312 | tf_op jit(solution)/shard_map/ppermute | solution.py:229
  126.8 11.0 %collective-permute-start.28 = (bf16[16,128]{1,0:T(8,128)(2,1)}, bf16[16,128]{1,0:T(8,128)(2,1)}, u32[]{:S(2)}, u32[]{:S(2)}) collective-permute-start(bf16[16,128]{1,0:T(8,128)(2,1)} %get-tuple-element.203), channel_id=1, source_target_pairs={{32,96},{33,97},{34,98},{35,99},{36,100},{37,101},{38,102},{39,103... | collective-permute-start | bytes 12296 | tf_op jit(solution)/shard_map/ppermute | solution.py:229
  145.5 5.8 %collective-permute-start.29 = (bf16[64,1152]{1,0:T(8,128)(2,1)}, bf16[64,1152]{1,0:T(8,128)(2,1)}, u32[]{:S(2)}, u32[]{:S(2)}) collective-permute-start(bf16[64,1152]{1,0:T(8,128)(2,1)} %get-tuple-element.206), channel_id=1, source_target_pairs={{0,32},{1,33},{2,34},{3,35},{4,36},{5,37},{6,38},{7,39},{8,40},{9,... | collective-permute-start | bytes 442376 | tf_op jit(solution)/shard_map/ppermute | solution.py:229
  146.8 4.4 %collective-permute-start.30 = (bf16[64,256]{1,0:T(8,128)(2,1)}, bf16[64,256]{1,0:T(8,128)(2,1)}, u32[]{:S(2)}, u32[]{:S(2)}) collective-permute-start(bf16[64,256]{1,0:T(8,128)(2,1)} %get-tuple-element.207), channel_id=1, source_target_pairs={{0,33},{1,34},{2,35},{3,36},{4,37},{5,38},{6,39},{7,40},{8,41},{9,... | collective-permute-start | bytes 98312 | tf_op jit(solution)/shard_map/ppermute | solution.py:229
  148.0 3.2 collective-permute-start.31
  157.4 5.8 %collective-permute-start.33 = (bf16[64,1152]{1,0:T(8,128)(2,1)}, bf16[64,1152]{1,0:T(8,128)(2,1)}, u32[]{:S(2)}, u32[]{:S(2)}) collective-permute-start(bf16[64,1152]{1,0:T(8,128)(2,1)} %get-tuple-element.212), channel_id=1, source_target_pairs={{32,64},{33,65},{34,66},{35,67},{36,68},{37,69},{38,70},{39,71},{4... | collective-permute-start | bytes 442376 | tf_op jit(solution)/shard_map/ppermute | solution.py:229
  158.7 4.4 %collective-permute-start.34 = (bf16[64,256]{1,0:T(8,128)(2,1)}, bf16[64,256]{1,0:T(8,128)(2,1)}, u32[]{:S(2)}, u32[]{:S(2)}) collective-permute-start(bf16[64,256]{1,0:T(8,128)(2,1)} %get-tuple-element.213), channel_id=1, source_target_pairs={{32,65},{33,66},{34,67},{35,68},{36,69},{37,70},{38,71},{39,72},{4... | collective-permute-start | bytes 98312 | tf_op jit(solution)/shard_map/ppermute | solution.py:229
  159.9 3.2 collective-permute-start.35
  169.3 17.0 %collective-permute-start.37 = (bf16[64,1152]{1,0:T(8,128)(2,1)}, bf16[64,1152]{1,0:T(8,128)(2,1)}, u32[]{:S(2)}, u32[]{:S(2)}) collective-permute-start(bf16[64,1152]{1,0:T(8,128)(2,1)} %get-tuple-element.218), channel_id=1, source_target_pairs={{64,96},{65,97},{66,98},{67,99},{68,100},{69,101},{70,102},{71,103... | collective-permute-start | bytes 442376 | tf_op jit(solution)/shard_map/ppermute | solution.py:229
  170.6 14.5 %collective-permute-start.38 = (bf16[64,256]{1,0:T(8,128)(2,1)}, bf16[64,256]{1,0:T(8,128)(2,1)}, u32[]{:S(2)}, u32[]{:S(2)}) collective-permute-start(bf16[64,256]{1,0:T(8,128)(2,1)} %get-tuple-element.219), channel_id=1, source_target_pairs={{64,97},{65,98},{66,99},{67,100},{68,101},{69,102},{70,103},{71,10... | collective-permute-start | bytes 98312 | tf_op jit(solution)/shard_map/ppermute | solution.py:229
  171.9 14.4 %collective-permute-start.39 = (bf16[64,256]{1,0:T(8,128)(2,1)}, bf16[64,256]{1,0:T(8,128)(2,1)}, u32[]{:S(2)}, u32[]{:S(2)}) collective-permute-start(bf16[64,256]{1,0:T(8,128)(2,1)} %get-tuple-element.220), channel_id=1, source_target_pairs={{65,96},{66,97},{67,98},{68,99},{69,100},{70,101},{71,102},{72,103... | collective-permute-start | bytes 98312 | tf_op jit(solution)/shard_map/ppermute | solution.py:229
  173.2 11.2 %collective-permute-start.40 = (bf16[16,128]{1,0:T(8,128)(2,1)}, bf16[16,128]{1,0:T(8,128)(2,1)}, u32[]{:S(2)}, u32[]{:S(2)}) collective-permute-start(bf16[16,128]{1,0:T(8,128)(2,1)} %get-tuple-element.221), channel_id=1, source_target_pairs={{32,96},{33,97},{34,98},{35,99},{36,100},{37,101},{38,102},{39,103... | collective-permute-start | bytes 12296 | tf_op jit(solution)/shard_map/ppermute | solution.py:229
  192.4 5.8 %collective-permute-start.41 = (bf16[64,1152]{1,0:T(8,128)(2,1)}, bf16[64,1152]{1,0:T(8,128)(2,1)}, u32[]{:S(2)}, u32[]{:S(2)}) collective-permute-start(bf16[64,1152]{1,0:T(8,128)(2,1)} %get-tuple-element.224), channel_id=1, source_target_pairs={{0,32},{1,33},{2,34},{3,35},{4,36},{5,37},{6,38},{7,39},{8,40},{9,... | collective-permute-start | bytes 442376 | tf_op jit(solution)/shard_map/ppermute | solution.py:229
  193.7 4.4 %collective-permute-start.42 = (bf16[64,256]{1,0:T(8,128)(2,1)}, bf16[64,256]{1,0:T(8,128)(2,1)}, u32[]{:S(2)}, u32[]{:S(2)}) collective-permute-start(bf16[64,256]{1,0:T(8,128)(2,1)} %get-tuple-element.225), channel_id=1, source_target_pairs={{0,33},{1,34},{2,35},{3,36},{4,37},{5,38},{6,39},{7,40},{8,41},{9,... | collective-permute-start | bytes 98312 | tf_op jit(solution)/shard_map/ppermute | solution.py:229
  195.0 3.2 collective-permute-start.43
  196.2 1.2 collective-permute-start.44
  204.3 5.8 %collective-permute-start.45 = (bf16[64,1152]{1,0:T(8,128)(2,1)}, bf16[64,1152]{1,0:T(8,128)(2,1)}, u32[]{:S(2)}, u32[]{:S(2)}) collective-permute-start(bf16[64,1152]{1,0:T(8,128)(2,1)} %get-tuple-element.230), channel_id=1, source_target_pairs={{32,64},{33,65},{34,66},{35,67},{36,68},{37,69},{38,70},{39,71},{4... | collective-permute-start | bytes 442376 | tf_op jit(solution)/shard_map/ppermute | solution.py:229
  205.6 4.4 %collective-permute-start.46 = (bf16[64,256]{1,0:T(8,128)(2,1)}, bf16[64,256]{1,0:T(8,128)(2,1)}, u32[]{:S(2)}, u32[]{:S(2)}) collective-permute-start(bf16[64,256]{1,0:T(8,128)(2,1)} %get-tuple-element.231), channel_id=1, source_target_pairs={{32,65},{33,66},{34,67},{35,68},{36,69},{37,70},{38,71},{39,72},{4... | collective-permute-start | bytes 98312 | tf_op jit(solution)/shard_map/ppermute | solution.py:229
  206.9 3.2 collective-permute-start.47
  208.1 1.2 collective-permute-start.48
  216.2 15.9 %collective-permute-start.49 = (bf16[64,1152]{1,0:T(8,128)(2,1)}, bf16[64,1152]{1,0:T(8,128)(2,1)}, u32[]{:S(2)}, u32[]{:S(2)}) collective-permute-start(bf16[64,1152]{1,0:T(8,128)(2,1)} %get-tuple-element.236), channel_id=1, source_target_pairs={{64,96},{65,97},{66,98},{67,99},{68,100},{69,101},{70,102},{71,103... | collective-permute-start | bytes 442376 | tf_op jit(solution)/shard_map/ppermute | solution.py:229
  217.5 13.4 %collective-permute-start.50 = (bf16[64,256]{1,0:T(8,128)(2,1)}, bf16[64,256]{1,0:T(8,128)(2,1)}, u32[]{:S(2)}, u32[]{:S(2)}) collective-permute-start(bf16[64,256]{1,0:T(8,128)(2,1)} %get-tuple-element.237), channel_id=1, source_target_pairs={{64,97},{65,98},{66,99},{67,100},{68,101},{69,102},{70,103},{71,10... | collective-permute-start | bytes 98312 | tf_op jit(solution)/shard_map/ppermute | solution.py:229
  218.8 13.4 %collective-permute-start.51 = (bf16[64,256]{1,0:T(8,128)(2,1)}, bf16[64,256]{1,0:T(8,128)(2,1)}, u32[]{:S(2)}, u32[]{:S(2)}) collective-permute-start(bf16[64,256]{1,0:T(8,128)(2,1)} %get-tuple-element.238), channel_id=1, source_target_pairs={{65,96},{66,97},{67,98},{68,99},{69,100},{70,101},{71,102},{72,103... | collective-permute-start | bytes 98312 | tf_op jit(solution)/shard_map/ppermute | solution.py:229
  220.1 10.1 %collective-permute-start.52 = (bf16[16,128]{1,0:T(8,128)(2,1)}, bf16[16,128]{1,0:T(8,128)(2,1)}, u32[]{:S(2)}, u32[]{:S(2)}) collective-permute-start(bf16[16,128]{1,0:T(8,128)(2,1)} %get-tuple-element.239), channel_id=1, source_target_pairs={{32,96},{33,97},{34,98},{35,99},{36,100},{37,101},{38,102},{39,103... | collective-permute-start | bytes 12296 | tf_op jit(solution)/shard_map/ppermute | solution.py:229
  238.3 5.8 %collective-permute-start.53 = (bf16[64,1152]{1,0:T(8,128)(2,1)}, bf16[64,1152]{1,0:T(8,128)(2,1)}, u32[]{:S(2)}, u32[]{:S(2)}) collective-permute-start(bf16[64,1152]{1,0:T(8,128)(2,1)} %get-tuple-element.242), channel_id=1, source_target_pairs={{0,32},{1,33},{2,34},{3,35},{4,36},{5,37},{6,38},{7,39},{8,40},{9,... | collective-permute-start | bytes 442376 | tf_op jit(solution)/shard_map/ppermute | solution.py:229
  239.6 4.4 %collective-permute-start.54 = (bf16[64,256]{1,0:T(8,128)(2,1)}, bf16[64,256]{1,0:T(8,128)(2,1)}, u32[]{:S(2)}, u32[]{:S(2)}) collective-permute-start(bf16[64,256]{1,0:T(8,128)(2,1)} %get-tuple-element.243), channel_id=1, source_target_pairs={{0,33},{1,34},{2,35},{3,36},{4,37},{5,38},{6,39},{7,40},{8,41},{9,... | collective-permute-start | bytes 98312 | tf_op jit(solution)/shard_map/ppermute | solution.py:229
  240.8 3.2 collective-permute-start.55
  242.1 1.2 collective-permute-start.56
  250.4 5.8 %collective-permute-start.57 = (bf16[64,1152]{1,0:T(8,128)(2,1)}, bf16[64,1152]{1,0:T(8,128)(2,1)}, u32[]{:S(2)}, u32[]{:S(2)}) collective-permute-start(bf16[64,1152]{1,0:T(8,128)(2,1)} %get-tuple-element.248), channel_id=1, source_target_pairs={{32,64},{33,65},{34,66},{35,67},{36,68},{37,69},{38,70},{39,71},{4... | collective-permute-start | bytes 442376 | tf_op jit(solution)/shard_map/ppermute | solution.py:229
  251.7 4.4 %collective-permute-start.58 = (bf16[64,256]{1,0:T(8,128)(2,1)}, bf16[64,256]{1,0:T(8,128)(2,1)}, u32[]{:S(2)}, u32[]{:S(2)}) collective-permute-start(bf16[64,256]{1,0:T(8,128)(2,1)} %get-tuple-element.249), channel_id=1, source_target_pairs={{32,65},{33,66},{34,67},{35,68},{36,69},{37,70},{38,71},{39,72},{4... | collective-permute-start | bytes 98312 | tf_op jit(solution)/shard_map/ppermute | solution.py:229
  253.0 3.2 collective-permute-start.59
  254.2 1.2 collective-permute-start.60
  262.9 101.3 %collective-permute-start.61 = (bf16[64,1152]{1,0:T(8,128)(2,1)}, bf16[64,1152]{1,0:T(8,128)(2,1)}, u32[]{:S(2)}, u32[]{:S(2)}) collective-permute-start(bf16[64,1152]{1,0:T(8,128)(2,1)} %get-tuple-element.254), channel_id=1, source_target_pairs={{64,96},{65,97},{66,98},{67,99},{68,100},{69,101},{70,102},{71,103... | collective-permute-start | bytes 442376 | tf_op jit(solution)/shard_map/ppermute | solution.py:229
  264.2 100.0 %collective-permute-start.62 = (bf16[64,256]{1,0:T(8,128)(2,1)}, bf16[64,256]{1,0:T(8,128)(2,1)}, u32[]{:S(2)}, u32[]{:S(2)}) collective-permute-start(bf16[64,256]{1,0:T(8,128)(2,1)} %get-tuple-element.255), channel_id=1, source_target_pairs={{64,97},{65,98},{66,99},{67,100},{68,101},{69,102},{70,103},{71,10... | collective-permute-start | bytes 98312 | tf_op jit(solution)/shard_map/ppermute | solution.py:229
  265.5 98.7 %collective-permute-start.63 = (bf16[64,256]{1,0:T(8,128)(2,1)}, bf16[64,256]{1,0:T(8,128)(2,1)}, u32[]{:S(2)}, u32[]{:S(2)}) collective-permute-start(bf16[64,256]{1,0:T(8,128)(2,1)} %get-tuple-element.256), channel_id=1, source_target_pairs={{65,96},{66,97},{67,98},{68,99},{69,100},{70,101},{71,102},{72,103... | collective-permute-start | bytes 98312 | tf_op jit(solution)/shard_map/ppermute | solution.py:229
  266.8 84.7 %collective-permute-start.64 = (bf16[16,128]{1,0:T(8,128)(2,1)}, bf16[16,128]{1,0:T(8,128)(2,1)}, u32[]{:S(2)}, u32[]{:S(2)}) collective-permute-start(bf16[16,128]{1,0:T(8,128)(2,1)} %get-tuple-element.257), channel_id=1, source_target_pairs={{32,96},{33,97},{34,98},{35,99},{36,100},{37,101},{38,102},{39,103... | collective-permute-start | bytes 12296 | tf_op jit(solution)/shard_map/ppermute | solution.py:229
  372.3 18.1 %collective-permute-start.65 = (bf16[32,256]{1,0:T(8,128)(2,1)S(1)}, bf16[32,256]{1,0:T(8,128)(2,1)S(1)}, u32[]{:S(2)}, u32[]{:S(2)}) collective-permute-start(bf16[32,256]{1,0:T(8,128)(2,1)S(1)} %get-tuple-element.260), channel_id=1, source_target_pairs={{32,0},{64,32},{96,64},{128,96},{160,128},{192,160},{224,192},{256... | collective-permute-start | bytes 49160 | tf_op jit(solution)/shard_map/ppermute | solution.py:219
  373.6 4.4 %collective-permute-start.66 = (bf16[16,128]{1,0:T(8,128)(2,1)S(1)}, bf16[16,128]{1,0:T(8,128)(2,1)S(1)}, u32[]{:S(2)}, u32[]{:S(2)}) collective-permute-start(bf16[16,128]{1,0:T(8,128)(2,1)S(1)} %copy-done.94), channel_id=1, source_target_pairs={{64,96},{65,97},{66,98},{67,99},{68,100},{69,101},{70,102},{71,103... | collective-permute-start | bytes 12296 | tf_op jit(solution)/shard_map/ppermute | solution.py:229
  (99 other events, 187.2 us)

commit v2 on v1

v2 whole, which is shorter than its diff:
```python
import functools

import jax
import jax.numpy as jnp
from jax import lax
from jax.experimental import pallas as pl
from jax.experimental.pallas import tpu as pltpu
from jax.sharding import PartitionSpec as P

CELLS = 256
ROWS = 64
HALF = 32
SENT_ROWS = 144
LANES = 128
BF16 = jnp.bfloat16
F32 = jnp.float32
GRANT = 60 * 1024 * 1024


def row_dot(first, second):
    return lax.dot_general(first, second, (((1,), (1,)), ((), ())), preferred_element_type=F32)


def mat_dot(first, second):
    return jnp.dot(first, second, preferred_element_type=F32)


def turned(field):
    return jnp.concatenate([-field[HALF:], field[:HALF]], axis=0)


def coefficients(field, right):
    return row_dot(field[:HALF], right) + row_dot(field[HALF:], turned(right))


def packed(coeff):
    return jnp.concatenate([coeff[:16], coeff[16:]], axis=1)


def unpacked(dense):
    return jnp.concatenate([dense[:, :ROWS], dense[:, ROWS:]], axis=0)


def by_quarter(sums):
    return jnp.concatenate([unpacked(sums[q]) for q in range(4)], axis=1)


def seen(quarter, viewer):
    level = (lax.broadcasted_iota(jnp.int32, (ROWS, 1), 0) // 16) % 2
    far_half = jnp.where(viewer // 2 == quarter // 2, 0.0, 1.0).astype(F32)
    sibling = jnp.where(jnp.bitwise_xor(viewer, 1) == quarter, 1.0, 0.0).astype(F32)
    return jnp.where(level == 0, far_half, sibling)


def weights_of(basis):
    real, imag = basis[:HALF], basis[HALF:]
    return jnp.concatenate([real, -imag], axis=0), jnp.concatenate([imag, real], axis=0)


def far_rows(coeff, weights_ref):
    width = weights_ref.shape[1] // 2
    both = mat_dot(coeff, weights_ref[...])
    return jnp.concatenate([both[:, :width], both[:, width:]], axis=0)


def leaf_fetches(blocks_in, blocks, done):
    return [
        pltpu.make_async_copy(blocks_in.at[:, :, pl.ds(j * CELLS, CELLS)], blocks.at[j], done.at[j])
        for j in range(blocks.shape[0])
    ]


def near_leaf(leaf, leaves, own, lower, upper, blocks, total=None):
    below = own[leaf - 1] if leaf else lower
    above = own[leaf + 1] if leaf + 1 < leaves else upper
    for side, part in ((0, own[leaf]), (1, below), (2, above)):
        if part is None:
            continue
        term = row_dot(part, blocks[leaf, side, 0]) + row_dot(turned(part), blocks[leaf, side, 1])
        total = term if total is None else total + term
    return total


def own_quarter():
    per_quarter = lax.axis_size("leaf") // 4
    return lax.axis_index("leaf") // per_quarter


def prepare_kernel(ranks, field, left_parts, right_parts, coupling, left, basis, right, low_end, up_end):
    width = left.shape[1]
    mine = own_quarter()
    row = lax.broadcasted_iota(jnp.int32, (ROWS, 1), 0)
    limit = jnp.where((row // 16) % 2 == 0, ranks[0, mine // 2], ranks[0, 2 + mine])
    keep = jnp.where(row % 16 < limit, 1.0, 0.0).astype(F32)
    order = ((0, 0), (1, 0), (0, 1), (1, 1))
    stacked = jnp.concatenate([left_parts[level, part] for level, part in order], axis=0)
    kept = stacked.astype(F32) * keep
    left[...] = kept.astype(BF16)
    coupled = (kept * coupling[...].astype(F32)).astype(BF16)
    basis[...] = coupled
    right[...] = jnp.concatenate([right_parts[level, part] for level, part in order], axis=0)
    low_end[:ROWS] = field[:, :CELLS]
    low_end[ROWS:] = coupled[:, :CELLS]
    up_end[:ROWS] = field[:, width - CELLS :]
    up_end[ROWS:] = coupled[:, width - CELLS :]


def sums_kernel(field, basis, right, sums):
    sums[:16] = packed(coefficients(field[...], right[...])).astype(BF16)
    sums[16:] = packed(coefficients(basis[...], right[...])).astype(BF16)


def first_kernel(field, lower, upper, basis, ends, right_next, blocks_in, pack_out, pack, blocks, done):
    fetches = leaf_fetches(blocks_in, blocks, done)
    for fetch in fetches:
        fetch.start()
    width = field.shape[1]
    leaves = width // CELLS
    both = [
        jnp.concatenate([field[:, j * CELLS : (j + 1) * CELLS], basis[:, j * CELLS : (j + 1) * CELLS]], axis=0)
        for j in range(leaves)
    ]
    below = jnp.concatenate([lower[:ROWS], ends[:, :CELLS]], axis=0)
    above = jnp.concatenate([upper[:ROWS], ends[:, CELLS:]], axis=0)

    def product(part, leaf, side):
        spun = jnp.concatenate([turned(part[:ROWS]), turned(part[ROWS:])], axis=0)
        return row_dot(part, blocks[leaf, side, 0]) + row_dot(spun, blocks[leaf, side, 1])

    for j in range(leaves):
        fetches[j].wait()
        total = product(both[j], j, 0)
        for side, part, edge in (
            (1, both[j - 1] if j else below, j == 0), (2, both[j + 1] if j + 1 < leaves else above, j + 1 == leaves),
        ):
            term = product(part, j, side)
            if edge:
                at = 2 * width + (side - 1) * CELLS
                pack[:, at : at + CELLS] = term[ROWS:]
                term = jnp.concatenate([term[:ROWS], jnp.zeros((ROWS, CELLS), F32)], axis=0)
            total = total + term
        pack[:, j * CELLS : (j + 1) * CELLS] = total[:ROWS]
        pack[:, width + j * CELLS : width + (j + 1) * CELLS] = total[ROWS:]
    copy = pltpu.make_async_copy(pack, pack_out, done.at[leaves])
    copy.start()
    copy.wait()


def emit_field(value, coupling, right_next, carried, out, out_low, out_up, out_sums):
    width = value.shape[1]
    sent = (coupling * value).astype(BF16)
    out[:, :width] = sent
    out[:HALF, width:] = carried[:, :LANES]
    out[HALF:, width:] = carried[:, LANES:]
    out_low[...] = sent[:, :CELLS]
    out_up[...] = sent[:, width - CELLS :]
    out_sums[:16] = packed(coefficients(sent, right_next)).astype(BF16)


def second_kernel(
    all_sums, left, coupling, right_next, pack_in,
    value_out, base_out, left_out, weights_out, out, out_low, out_up, out_sums,
    pack, base, left_w, weights, done,
):
    fetch = pltpu.make_async_copy(pack_in, pack, done.at[0])
    fetch.start()
    width = left.shape[1]
    per_quarter = lax.axis_size("leaf") // 4
    leaf = lax.axis_index("leaf")
    mine = leaf // per_quarter
    low_view = (leaf + per_quarter - 1) // per_quarter - 1
    up_view = (leaf + 1) // per_quarter
    last = width - CELLS
    left_r, left_i = weights_of(left[...].astype(F32))
    for q in range(4):
        rows = slice(q * ROWS, (q + 1) * ROWS)
        own_mask = seen(q, mine)
        left_w[rows, :width] = (left_r * own_mask).astype(BF16)
        left_w[rows, width:] = (left_i * own_mask).astype(BF16)
    keep_left = pltpu.make_async_copy(left_w, left_out, done.at[1])
    keep_left.start()
    sums = jnp.sum(all_sums[...].astype(F32).reshape(4, -1, HALF, LANES), axis=1)
    coeff = by_quarter(sums[:, :16]).astype(BF16)
    far = far_rows(coeff, left_w)
    fetch.wait()
    value = pack[:, :width] + far
    base[:ROWS] = value
    base[ROWS:] = jnp.broadcast_to(coupling[...].astype(F32), (8, width))
    keep_base = pltpu.make_async_copy(base, base_out, done.at[2])
    keep_base.start()
    keep_value = pltpu.make_async_copy(base.at[:ROWS], value_out, done.at[3])
    keep_value.start()
    emit_field(
        value, coupling[...].astype(F32), right_next[...], jnp.zeros((HALF, 2 * LANES), BF16),
        out, out_low, out_up, out_sums,
    )
    ext_r, ext_i = weights_of(pack[:, width : 2 * width])
    low_r, low_i = weights_of(pack[:, 2 * width : 2 * width + CELLS])
    up_r, up_i = weights_of(pack[:, 2 * width + CELLS :])
    for q in range(4):
        rows = slice(q * ROWS, (q + 1) * ROWS)
        own_mask, low_mask, up_mask = seen(q, mine), seen(q, low_view), seen(q, up_view)
        for at, ext_p, low_p, up_p in ((0, ext_r, low_r, up_r), (width, ext_i, low_i, up_i)):
            ext_m = ext_p * own_mask
            weights[rows, at : at + CELLS] = (ext_m[:, :CELLS] + low_p * low_mask).astype(BF16)
            weights[rows, at + CELLS : at + last] = ext_m[:, CELLS:last].astype(BF16)
            weights[rows, at + last : at + width] = (ext_m[:, last:] + up_p * up_mask).astype(BF16)
    columns = []
    for q in range(4):
        real = unpacked(sums[q, 16:])
        imag = jnp.concatenate([-real[:, HALF:], real[:, :HALF]], axis=1)
        block = jnp.concatenate([real, imag], axis=0)
        columns.append(jnp.concatenate([block * seen(s, q) for s in range(4)], axis=0))
    weights[:, 2 * width :] = jnp.concatenate(columns, axis=1).astype(BF16)
    keep_weights = pltpu.make_async_copy(weights, weights_out, done.at[4])
    keep_weights.start()
    keep_left.wait()
    keep_base.wait()
    keep_value.wait()
    keep_weights.wait()


def turn_kernel(
    turn, field, lower, upper, all_sums, right_in, blocks_in, early, base_in, weights_in, old_value, old_coeff,
    value_out, coeff_out, field_out, low_out, up_out, sums_out,
    blocks, right_next, base, weights, value, coeff, sent, sent_low, sent_up, sent_sums, done,
):
    @pl.when(lax.axis_index("layer") == turn)
    def _():
        width = base.shape[1]
        leaves = width // CELLS
        leaf_parts = leaf_fetches(blocks_in, blocks, done)
        fetches = [
            pltpu.make_async_copy(source, target, done.at[leaves + number])
            for number, (source, target) in enumerate((
                (weights_in, weights), (base_in, base), (right_in, right_next),
            ))
        ]
        for fetch in leaf_parts + fetches:
            fetch.start()
        own = [field[:, j * CELLS : (j + 1) * CELLS] for j in range(leaves)]
        near = []
        for j in range(leaves):
            leaf_parts[j].wait()
            near.append(near_leaf(j, leaves, own, lower[...], upper[...], blocks))
        sums = jnp.sum(all_sums[...].astype(F32).reshape(4, -1, 16, LANES), axis=1)
        carried = jnp.concatenate([field[:HALF, width:], field[HALF:, width:]], axis=1)
        coeff[...] = (by_quarter(sums) - carried.astype(F32)).astype(BF16)
        fetches[0].wait()
        far = mat_dot(coeff[...], weights[...])
        fetches[1].wait()
        update = jnp.concatenate([far[:, :width], far[:, width : 2 * width]], axis=0)
        total = base[:ROWS] - jnp.concatenate(near, axis=1) + update
        value[...] = total
        onward = far[:, 2 * width :].astype(BF16)
        fetches[2].wait()
        emit_field(total, base[ROWS : ROWS + 1], right_next[...], onward, sent, sent_low, sent_up, sent_sums)
        keeps = [
            pltpu.make_async_copy(source, target, done.at[leaves + len(fetches) + number])
            for number, (source, target) in enumerate((
                (sent, field_out), (sent_low, low_out), (sent_up, up_out), (sent_sums, sums_out),
                (value, value_out), (coeff, coeff_out),
            ))
        ]
        for keep in keeps:
            keep.start()
        for keep in keeps:
            keep.wait()


def last_kernel(layers, received, all_sums, field_in, value_in, left_in, out, extras, value, left_w, done):
    width = value.shape[1]
    fetch_left = pltpu.make_async_copy(left_in, left_w, done.at[0])
    fetch_left.start()
    fetch_value = pltpu.make_async_copy(value_in, value, done.at[1])
    fetch_value.start()
    fetch_extras = pltpu.make_async_copy(field_in.at[:, width:], extras, done.at[2])
    fetch_extras.start()
    sums = jnp.sum(all_sums[...].astype(F32).reshape(4, -1, 16, LANES), axis=1)
    fetch_extras.wait()
    carried = jnp.concatenate([extras[:HALF], extras[HALF:]], axis=1).astype(F32)
    final = by_quarter(sums) - carried
    is_last = lax.axis_index("layer") == layers - 1
    coeff = jnp.where(is_last, final, received[...].astype(F32)).astype(BF16)
    fetch_left.wait()
    far = far_rows(coeff, left_w)
    fetch_value.wait()
    out[...] = (value[...] - far).astype(BF16)


def vmem(count):
    return [pl.BlockSpec(memory_space=pltpu.VMEM)] * count


def anywhere(count):
    return [pl.BlockSpec(memory_space=pl.ANY)] * count


def smem(count):
    return [pl.BlockSpec(memory_space=pltpu.SMEM)] * count


def shape(dims, dtype):
    return jax.ShapeDtypeStruct(dims, dtype)


def body(right_side, near_blocks, right_bases, left_bases, coupling, ranks):
    layer_count = lax.axis_size("layer")
    leaf_count = lax.axis_size("leaf")
    layer = lax.axis_index("layer")
    width = right_side.shape[3]
    field = right_side[0].reshape(ROWS, width)
    blocks = near_blocks[0]
    params = pltpu.CompilerParams(vmem_limit_bytes=GRANT)

    def beside(value, by):
        return lax.ppermute(value, "leaf", [(i, i + by) for i in range(leaf_count) if 0 <= i + by < leaf_count])

    def back(value):
        return lax.ppermute(value, "layer", [(i + 1, i) for i in range(layer_count - 1)])

    def ahead(value, turn, by, hop=1):
        pairs = [
            (k * leaf_count + i, (k + hop) * leaf_count + i + by)
            for k in range(layer_count - hop)
            if (k - turn) % 3 == 0
            for i in range(leaf_count)
            if 0 <= i + by < leaf_count
        ]
        return lax.ppermute(value, ("layer", "leaf"), pairs)

    def all_ahead(value, by):
        pairs = [
            (k * leaf_count + i, (k + 1) * leaf_count + i + by)
            for k in range(layer_count - 1)
            for i in range(leaf_count)
            if 0 <= i + by < leaf_count
        ]
        return lax.ppermute(value, ("layer", "leaf"), pairs)

    def to_all(value):
        copies = jnp.broadcast_to(value, (leaf_count, *value.shape))
        return lax.all_to_all(copies, "leaf", split_axis=0, concat_axis=0, tiled=True)

    def to_all_of(turn, value):
        return lax.cond(
            layer == turn, lambda v: to_all(v[:16]), lambda v: jnp.zeros((leaf_count, 16, LANES), v.dtype), value
        )

    left, basis, right, low_end, up_end = pl.pallas_call(
        prepare_kernel,
        out_shape=[shape((ROWS, width), BF16)] * 3 + [shape((2 * ROWS, CELLS), BF16)] * 2,
        in_specs=smem(1) + vmem(4), out_specs=vmem(5), compiler_params=params, name="prepare",
    )(ranks, field, left_bases[0], right_bases[0], coupling)
    lower = beside(up_end, 1)
    upper = beside(low_end, -1)
    basis_in = all_ahead(basis, 0)
    right_next = back(right)
    ends_in = all_ahead(jnp.concatenate([lower[ROWS:], upper[ROWS:]], axis=1), 0)
    sums = pl.pallas_call(
        sums_kernel, out_shape=shape((HALF, LANES), BF16),
        in_specs=vmem(3), out_specs=vmem(1)[0], compiler_params=params, name="sums",
    )(field, basis_in, right)
    all_sums = to_all(sums)
    packed_width = 2 * width + 2 * CELLS
    leaves = width // CELLS
    slabs_shape = (leaves, 3, 2, CELLS, CELLS)
    pack = pl.pallas_call(
        first_kernel,
        out_shape=shape((ROWS, packed_width), F32),
        in_specs=vmem(5) + anywhere(2), out_specs=anywhere(1)[0],
        scratch_shapes=[
            pltpu.VMEM((ROWS, packed_width), F32), pltpu.VMEM(slabs_shape, BF16), pltpu.SemaphoreType.DMA((leaves + 1,)),
        ],
        compiler_params=params, name="first",
    )(field, lower, upper, basis_in, ends_in, right_next, blocks)
    field_shapes = [
        shape((ROWS, width + LANES), BF16), shape((ROWS, CELLS), BF16), shape((ROWS, CELLS), BF16),
        shape((SENT_ROWS, LANES), BF16),
    ]
    base_shape, weights_shape = (ROWS + 8, width), (256, 2 * width + 256)
    value, base, left_w, weights, sent, sent_low, sent_up, sums = pl.pallas_call(
        second_kernel,
        out_shape=[
            shape((ROWS, width), F32), shape(base_shape, F32), shape((256, 2 * width), BF16),
            shape(weights_shape, BF16), *field_shapes,
        ],
        in_specs=vmem(4) + anywhere(1), out_specs=anywhere(4) + vmem(4),
        scratch_shapes=[
            pltpu.VMEM((ROWS, packed_width), F32), pltpu.VMEM(base_shape, F32), pltpu.VMEM((256, 2 * width), BF16),
            pltpu.VMEM(weights_shape, BF16), pltpu.SemaphoreType.DMA((5,)),
        ],
        compiler_params=params, name="second",
    )(all_sums, left, coupling, right_next, pack)

    coeff = jnp.zeros((HALF, 256), BF16)
    summed = jnp.zeros((leaf_count, 16, LANES), BF16)
    for turn in range(1, layer_count):
        early = ahead(sums, turn - 1, 0, 1 if turn == layer_count - 1 else 2)
        got = ahead(sent, turn - 1, 0)
        got_low = ahead(sent_up, turn - 1, 1)
        got_up = ahead(sent_low, turn - 1, -1)
        value, coeff, sent, sent_low, sent_up, sums = pl.pallas_call(
            functools.partial(turn_kernel, turn),
            out_shape=[shape((ROWS, width), F32), shape((HALF, 256), BF16), *field_shapes],
            in_specs=vmem(4) + anywhere(7), out_specs=anywhere(6),
            scratch_shapes=[
                pltpu.VMEM(slabs_shape, BF16), pltpu.VMEM((ROWS, width), BF16), pltpu.VMEM(base_shape, F32), pltpu.VMEM(weights_shape, BF16), pltpu.VMEM((ROWS, width), F32), pltpu.VMEM((HALF, 256), BF16),
                *[pltpu.VMEM(item.shape, item.dtype) for item in field_shapes], pltpu.SemaphoreType.DMA((leaves + 9,)),
            ],
            input_output_aliases={9: 0, 10: 1}, compiler_params=params, name="turn",
        )(got, got_low, got_up, summed, right_next, blocks, early, base, weights, value, coeff)
        summed = to_all_of(min(turn + 1, layer_count - 1), early)
    out = pl.pallas_call(
        functools.partial(last_kernel, layer_count),
        out_shape=shape((ROWS, width), BF16),
        in_specs=vmem(2) + anywhere(3), out_specs=vmem(1)[0],
        scratch_shapes=[
            pltpu.VMEM((ROWS, LANES), BF16), pltpu.VMEM((ROWS, width), F32), pltpu.VMEM((256, 2 * width), BF16),
            pltpu.SemaphoreType.DMA((3,)),
        ],
        compiler_params=params, name="last",
    )(back(coeff), summed, sent, value, left_w)
    return out.reshape(2, HALF, width)[None]


def solution(mesh):
    placed = (
        P("layer", None, None, "leaf"),
        P("layer", None, None, "leaf", None),
        P("layer", None, None, None, "leaf"),
        P("layer", None, None, None, "leaf"),
        P("layer", "leaf"),
        P("layer", None),
    )
    return jax.shard_map(
        body, mesh=mesh, in_specs=placed, out_specs=P("layer", None, None, "leaf"), check_vma=False
    )
```

time: 399 us -> 310 us (0.78)
  local copies, waits for them, and re-layouts: 89 us -> 14.8 us
  starting transfers between devices: 100 us -> 73.7 us
  waiting for transfers between devices: 141 us -> 156 us
  other arithmetic: 4.65 us -> 0.01 us
    unnamed x191 -> x104, local copies, waits for them, and re-layouts: 77.1 us -> 11.8 us
    ppermute x60, starting transfers between devices: 74.7 us -> 53.1 us  [ahead(): return lax.ppermute(value, ('layer', 'leaf'), pairs)]
    ppermute x60, waiting for transfers between devices: 136 us -> 146 us  [ahead(): return lax.ppermute(value, ('layer', 'leaf'), pairs)]
    ppermute x3 -> x2, waiting for transfers between devices: 0.01 us -> 8.86 us  [all_ahead(): return lax.ppermute(value, ('layer', 'leaf'), pairs)]
    another operation x14, local copies, waits for them, and re-layouts: 8.77 us -> 0.95 us
    pallas_call x17 -> x19, Pallas kernels: 31.8 us -> 32.8 us  [the longest x15 20.7 us: body(): pl.pallas_call(functools.partial(turn_kernel, turn), out_shape=[shape((RO...]
  transfers between devices with their start and end apart: 68 -> 67, of which waited for: 13 -> 16; matrix products, arithmetic and copies ran while one was open for 3% -> 0% of each run, Pallas kernels for 0% -> 2%
where the time goes in v2:
time: 310 us; the launch traced here: 308 us
  waiting for transfers between devices  156 us (50%)
  starting transfers between devices  73.7 us (24%)
  Pallas kernels  37.3 us (12%)
  blocking collectives  24.1 us (8%)
  local copies, waits for them, and re-layouts  14.8 us (5%)
    ppermute x60, waiting for transfers between devices, ahead(): return lax.ppermute(value, ('layer', 'leaf'), pairs)  146 us
    ppermute x60, starting transfers between devices, ahead(): return lax.ppermute(value, ('layer', 'leaf'), pairs)  53.1 us
    all_to_all x2, blocking collectives, to_all(): lax.all_to_all(copies, 'leaf', split_axis=0, concat_axis=0, tiled=True)  24.1 us
    pallas_call x15, Pallas kernels, body(): pl.pallas_call(functools.partial(turn_kernel, turn), out_shape=[shape((RO...  20.7 us
    unnamed x104, local copies, waits for them, and re-layouts  11.8 us
    ppermute x2, waiting for transfers between devices, all_ahead(): return lax.ppermute(value, ('layer', 'leaf'), pairs)  8.86 us
    all_to_all x1, starting transfers between devices, to_all(): lax.all_to_all(copies, 'leaf', split_axis=0, concat_axis=0, tiled=True)  8.63 us
  transfers between devices with their start and end apart: 67, of which 16 were waited for; matrix products, arithmetic and copies ran while one was open for 0% of the time, Pallas kernels for 2%

profile of v2, /device:TPU:481, one launch (start us, length us, event | category | flops | bytes accessed | tf_op | source)
XLA Modules:
  0.0 308.3 jit_solution(7566720506792765065)
XLA Ops:
  0.0 1.9 prepare.1
  1.9 1.3 collective-permute-start
  3.2 5.2 %collective-permute-done.basis = bf16[64,1024]{1,0:T(8,128)(2,1)S(1)} collective-permute-done((bf16[64,1024]{1,0:T(8,128)(2,1)}, bf16[64,1024]{1,0:T(8,128)(2,1)S(1)}, u32[]{:S(2)}, u32[]{:S(2)}) %collective-permute-start) | collective-permute-done | bytes 131104 | tf_op jit(solution)/shard_map/ppermute | solution.py:339
  9.0 2.0 sums.1
  11.0 1.4 broadcast_in_dim.51
  12.4 8.6 %all-to-all-start.15 = ((bf16[32,32,128]{2,1,0:T(8,128)(2,1)}), bf16[32,32,128]{2,1,0:T(8,128)(2,1)S(1)}, u32[]{:S(2)}, u32[]{:S(2)}) async-start(bf16[32,32,128]{2,1,0:T(8,128)(2,1)} %broadcast_in_dim.51), calls=%async_computation.15 | async-start | bytes 524288 | tf_op jit(solution)/shard_map/all_to_all | solution.py:343
  21.0 3.5 %collective-permute-start.2 = (bf16[128,256]{1,0:T(8,128)(2,1)}, bf16[128,256]{1,0:T(8,128)(2,1)S(1)}, u32[]{:S(2)}, u32[]{:S(2)}) collective-permute-start(bf16[128,256]{1,0:T(8,128)(2,1)} %get-tuple-element.168), channel_id=1, source_target_pairs={{0,1},{1,2},{2,3},{3,4},{4,5},{5,6},{6,7},{7,8},{8,9},{9,10},{10,1... | collective-permute-start | bytes 196616 | tf_op jit(solution)/shard_map/ppermute | solution.py:317
  24.6 1.9 collective-permute-start.3
  26.5 2.6 collective-permute-start.1
  29.2 1.2 collective-permute-done.3.upper
  30.4 1.3 collective-permute-start.4
  31.7 3.7 %collective-permute-done.4.ends = bf16[64,512]{1,0:T(8,128)(2,1)S(1)} collective-permute-done((bf16[64,512]{1,0:T(8,128)(2,1)S(1)}, bf16[64,512]{1,0:T(8,128)(2,1)S(1)}, u32[]{:S(2)}, u32[]{:S(2)}) %collective-permute-start.4) | collective-permute-done | bytes 65568 | tf_op jit(solution)/shard_map/ppermute | solution.py:339
  36.0 5.3 %first.1.pack_in = f32[64,2560]{1,0:T(8,128)} custom-call(bf16[64,1024]{1,0:T(8,128)(2,1)} %bitcast.23, bf16[128,256]{1,0:T(8,128)(2,1)} %copy-done.3, bf16[128,256]{1,0:T(8,128)(2,1)} %copy-done.4, bf16[64,1024]{1,0:T(8,128)(2,1)} %copy-done.2, bf16[64,512]{1,0:T(8,128)(2,1)} %copy-done.20, bf16[64,1024]{1,0:T(8,128)(2,1)} %copy-done, ...), custom_call_target="tpu_custom_call" | custom-call | tf_op jit(solution)/shard_map/first/pallas_call | solution.py:368
  42.0 4.4 %second.1 = (f32[64,1024]{1,0:T(8,128)}, f32[72,1024]{1,0:T(8,128)}, bf16[256,2048]{1,0:T(8,128)(2,1)}, bf16[256,2304]{1,0:T(8,128)(2,1)}, bf16[64,1152]{1,0:T(8...) custom-call(bf16[32,32,128]{2,1,0:T(8,128)(2,1)} %copy-done.1, ...), custom_call_target="tpu_custom_call" | custom-call | tf_op jit(solution)/shard_map/second/pallas_call | solution.py:382
  50.5 1.1 turn.15
  52.4 1.3 collective-permute-start.12
  55.1 13.7 %collective-permute-done.12.early = bf16[144,128]{1,0:T(8,128)(2,1)S(1)} collective-permute-done((bf16[144,128]{1,0:T(8,128)(2,1)}, bf16[144,128]{1,0:T(8,128)(2,1)S(1)}, u32[]{:S(2)}, u32[]{:S(2)}) %collective-permute-start.12) | collective-permute-done | bytes 36896 | tf_op jit(solution)/shard_map/ppermute | solution.py:330
  69.5 1.1 turn.16
  70.6 1.3 collective-permute-start.13
  72.5 1.3 collective-permute-start.14
  73.8 1.3 collective-permute-start.15
  75.2 3.8 %collective-permute-done.14.lower = bf16[64,256]{1,0:T(8,128)(2,1)S(1)} collective-permute-done((bf16[64,256]{1,0:T(8,128)(2,1)}, bf16[64,256]{1,0:T(8,128)(2,1)S(1)}, u32[]{:S(2)}, u32[]{:S(2)}) %collective-permute-start.14) | collective-permute-done | bytes 32800 | tf_op jit(solution)/shard_map/ppermute | solution.py:330
  79.0 2.1 collective-permute-done.15.upper
  81.8 1.1 turn.17
  88.1 1.3 collective-permute-start.24
  90.8 10.2 %collective-permute-done.24.early = bf16[144,128]{1,0:T(8,128)(2,1)S(1)} collective-permute-done((bf16[144,128]{1,0:T(8,128)(2,1)}, bf16[144,128]{1,0:T(8,128)(2,1)S(1)}, u32[]{:S(2)}, u32[]{:S(2)}) %collective-permute-start.24) | collective-permute-done | bytes 36896 | tf_op jit(solution)/shard_map/ppermute | solution.py:330
  101.7 1.1 turn.19
  102.8 1.3 collective-permute-start.25
  104.7 1.3 collective-permute-start.26
  106.0 1.3 collective-permute-start.27
  107.4 6.2 %collective-permute-done.26.lower = bf16[64,256]{1,0:T(8,128)(2,1)S(1)} collective-permute-done((bf16[64,256]{1,0:T(8,128)(2,1)}, bf16[64,256]{1,0:T(8,128)(2,1)S(1)}, u32[]{:S(2)}, u32[]{:S(2)}) %collective-permute-start.26) | collective-permute-done | bytes 32800 | tf_op jit(solution)/shard_map/ppermute | solution.py:330
  113.6 2.2 collective-permute-done.27.upper
  116.6 1.1 turn.20
  121.1 1.1 turn.21
  122.9 1.3 collective-permute-start.36
  125.6 13.7 %collective-permute-done.36.early = bf16[144,128]{1,0:T(8,128)(2,1)S(1)} collective-permute-done((bf16[144,128]{1,0:T(8,128)(2,1)}, bf16[144,128]{1,0:T(8,128)(2,1)S(1)}, u32[]{:S(2)}, u32[]{:S(2)}) %collective-permute-start.36) | collective-permute-done | bytes 36896 | tf_op jit(solution)/shard_map/ppermute | solution.py:330
  140.0 1.1 turn.22
  141.1 1.3 collective-permute-start.37
  143.0 1.3 collective-permute-start.38
  144.3 1.3 collective-permute-start.39
  145.7 5.0 %collective-permute-done.38.lower = bf16[64,256]{1,0:T(8,128)(2,1)S(1)} collective-permute-done((bf16[64,256]{1,0:T(8,128)(2,1)}, bf16[64,256]{1,0:T(8,128)(2,1)S(1)}, u32[]{:S(2)}, u32[]{:S(2)}) %collective-permute-start.38) | collective-permute-done | bytes 32800 | tf_op jit(solution)/shard_map/ppermute | solution.py:330
  150.7 1.9 collective-permute-done.39.upper
  157.8 1.1 turn.24
  159.5 1.3 collective-permute-start.48
  162.3 12.0 %collective-permute-done.48.early = bf16[144,128]{1,0:T(8,128)(2,1)S(1)} collective-permute-done((bf16[144,128]{1,0:T(8,128)(2,1)}, bf16[144,128]{1,0:T(8,128)(2,1)S(1)}, u32[]{:S(2)}, u32[]{:S(2)}) %collective-permute-start.48) | collective-permute-done | bytes 36896 | tf_op jit(solution)/shard_map/ppermute | solution.py:330
  176.1 1.3 collective-permute-start.49
  178.0 1.3 collective-permute-start.50
  179.3 1.3 collective-permute-start.51
  180.7 4.5 %collective-permute-done.50.lower = bf16[64,256]{1,0:T(8,128)(2,1)S(1)} collective-permute-done((bf16[64,256]{1,0:T(8,128)(2,1)}, bf16[64,256]{1,0:T(8,128)(2,1)S(1)}, u32[]{:S(2)}, u32[]{:S(2)}) %collective-permute-start.50) | collective-permute-done | bytes 32800 | tf_op jit(solution)/shard_map/ppermute | solution.py:330
  185.2 1.5 collective-permute-done.51.upper
  192.2 1.1 turn.27
  193.9 1.3 collective-permute-start.60
  196.7 69.0 %collective-permute-done.60.early = bf16[144,128]{1,0:T(8,128)(2,1)S(1)} collective-permute-done((bf16[144,128]{1,0:T(8,128)(2,1)}, bf16[144,128]{1,0:T(8,128)(2,1)S(1)}, u32[]{:S(2)}, u32[]{:S(2)}) %collective-permute-start.60) | collective-permute-done | bytes 36896 | tf_op jit(solution)/shard_map/ppermute | solution.py:330
  267.4 1.3 collective-permute-start.61
  268.7 1.3 collective-permute-start.64
  270.0 1.3 collective-permute-start.62
  271.3 1.3 collective-permute-start.63
  272.6 12.6 %conditional.28 = (bf16[32,16,128]{2,1,0:T(8,128)(2,1)S(1)}) conditional(s32[]{:T(128)} %convert_element_type.56, () %tuple.108, bf16[144,128]{1,0:T(8,128)(2,1)S(1)} %collective-permute-done.60.early), branch_computations={%region_26.0_spmd, %region_27.0_spmd} | conditional | bytes 405512 | solution.py:346
  272.6 12.5 %all_to_all.78 = bf16[32,16,128]{2,1,0:T(8,128)(2,1)S(1)} all-to-all(bf16[32,16,128]{2,1,0:T(8,128)(2,1)S(1)} %broadcast_in_dim.47), channel_id=1, replica_groups=mesh['layer'=16,'leaf'=32] {'leaf'}, dimensions={0} | all-to-all | bytes 262144 | tf_op jit(solution)/shard_map/cond/branch_1_fun/all_to_all | solution.py:343
  285.9 5.7 %turn.29 = (f32[64,1024]{1,0:T(8,128)}, bf16[32,256]{1,0:T(8,128)(2,1)}, bf16[64,1152]{1,0:T(8,128)(2,1)}, bf16[64,256]{1,0:T(8,128)(2,1)}, bf16[64,256]{1,0:T(8,128)(2,1)}, /*index=5*/bf16[144,128]{1,0:T(8,128)(2,1)}) custom-call(bf16[64,1152]{1,0:T(8,128)(2,1)} %copy-done.6, ...), custom_call_target="tpu_custom_call", output_to_operand_aliasing={{0}: (9, {}), {1}: (10, {})} | custom-call | tf_op jit(solution)/shard_map/turn/pallas_call | solution.py:403
  291.6 1.3 collective-permute-start.65
  292.9 11.6 %conditional.29 = (bf16[32,16,128]{2,1,0:T(8,128)(2,1)S(1)}) conditional(s32[]{:T(128)} %convert_element_type.56, () %tuple.109, bf16[144,128]{1,0:T(8,128)(2,1)S(1)} %collective-permute-done.64.early), branch_computations={%region_28.0_spmd, %region_29.0_spmd} | conditional | bytes 405512 | solution.py:346
  292.9 11.6 %all_to_all.79 = bf16[32,16,128]{2,1,0:T(8,128)(2,1)S(1)} all-to-all(bf16[32,16,128]{2,1,0:T(8,128)(2,1)S(1)} %broadcast_in_dim.48), channel_id=1, replica_groups=mesh['layer'=16,'leaf'=32] {'leaf'}, dimensions={0} | all-to-all | bytes 262144 | tf_op jit(solution)/shard_map/cond/branch_1_fun/all_to_all | solution.py:343
  305.1 3.0 last.1
  (234 shorter events, 45.6 us)
Async XLA Ops:
  1.9 6.5 %collective-permute-start = (bf16[64,1024]{1,0:T(8,128)(2,1)}, bf16[64,1024]{1,0:T(8,128)(2,1)S(1)}, u32[]{:S(2)}, u32[]{:S(2)}) collective-permute-start(bf16[64,1024]{1,0:T(8,128)(2,1)} %get-tuple-element.165), channel_id=1, source_target_pairs={{0,32},{1,33},{2,34},{3,35},{4,36},{5,37},{6,38},{7,39},{8,40},{9,... | collective-permute-start | bytes 393224 | tf_op jit(solution)/shard_map/ppermute | solution.py:339
  12.4 28.9 %all-to-all-start.15 = ((bf16[32,32,128]{2,1,0:T(8,128)(2,1)}), bf16[32,32,128]{2,1,0:T(8,128)(2,1)S(1)}, u32[]{:S(2)}, u32[]{:S(2)}) async-start(bf16[32,32,128]{2,1,0:T(8,128)(2,1)} %broadcast_in_dim.51), calls=%async_computation.15 | async-start | bytes 524288 | tf_op jit(solution)/shard_map/all_to_all | solution.py:343
  21.0 8.1 %collective-permute-start.2 = (bf16[128,256]{1,0:T(8,128)(2,1)}, bf16[128,256]{1,0:T(8,128)(2,1)S(1)}, u32[]{:S(2)}, u32[]{:S(2)}) collective-permute-start(bf16[128,256]{1,0:T(8,128)(2,1)} %get-tuple-element.168), channel_id=1, source_target_pairs={{0,1},{1,2},{2,3},{3,4},{4,5},{5,6},{6,7},{7,8},{8,9},{9,10},{10,1... | collective-permute-start | bytes 196616 | tf_op jit(solution)/shard_map/ppermute | solution.py:317
  24.6 5.8 %collective-permute-start.3 = (bf16[128,256]{1,0:T(8,128)(2,1)}, bf16[128,256]{1,0:T(8,128)(2,1)S(1)}, u32[]{:S(2)}, u32[]{:S(2)}) collective-permute-start(bf16[128,256]{1,0:T(8,128)(2,1)} %get-tuple-element.169), channel_id=1, source_target_pairs={{1,0},{2,1},{3,2},{4,3},{5,4},{6,5},{7,6},{8,7},{9,8},{10,9},{11,1... | collective-permute-start | bytes 196616 | tf_op jit(solution)/shard_map/ppermute | solution.py:317
  26.5 5.2 %collective-permute-start.1 = (bf16[64,1024]{1,0:T(8,128)(2,1)}, bf16[64,1024]{1,0:T(8,128)(2,1)S(1)}, u32[]{:S(2)}, u32[]{:S(2)}) collective-permute-start(bf16[64,1024]{1,0:T(8,128)(2,1)} %get-tuple-element.166.right), channel_id=1, source_target_pairs={{32,0},{64,32},{96,64},{128,96},{160,128},{192,160},{224,192},{256... | collective-permute-start | bytes 393224 | tf_op jit(solution)/shard_map/ppermute | solution.py:320
  30.4 5.0 %collective-permute-start.4 = (bf16[64,512]{1,0:T(8,128)(2,1)S(1)}, bf16[64,512]{1,0:T(8,128)(2,1)S(1)}, u32[]{:S(2)}, u32[]{:S(2)}) collective-permute-start(bf16[64,512]{1,0:T(8,128)(2,1)S(1)} %pad_maximum_fusion), channel_id=1, source_target_pairs={{0,32},{1,33},{2,34},{3,35},{4,36},{5,37},{6,38},{7,39},{8,40},{9,... | collective-permute-start | bytes 196616 | tf_op jit(solution)/shard_map/ppermute | solution.py:339
  46.5 2.7 collective-permute-start.5
  47.2 2.1 collective-permute-start.8
  47.8 1.3 collective-permute-start.6
  51.7 17.1 %collective-permute-start.9 = (bf16[64,1152]{1,0:T(8,128)(2,1)}, bf16[64,1152]{1,0:T(8,128)(2,1)S(1)}, u32[]{:S(2)}, u32[]{:S(2)}) collective-permute-start(bf16[64,1152]{1,0:T(8,128)(2,1)} %get-tuple-element.177), channel_id=1, source_target_pairs={{32,64},{33,65},{34,66},{35,67},{36,68},{37,69},{38,70},{39,71},{4... | collective-permute-start | bytes 442376 | tf_op jit(solution)/shard_map/ppermute | solution.py:330
  52.4 16.4 %collective-permute-start.12 = (bf16[144,128]{1,0:T(8,128)(2,1)}, bf16[144,128]{1,0:T(8,128)(2,1)S(1)}, u32[]{:S(2)}, u32[]{:S(2)}) collective-permute-start(bf16[144,128]{1,0:T(8,128)(2,1)} %get-tuple-element.180), channel_id=1, source_target_pairs={{32,96},{33,97},{34,98},{35,99},{36,100},{37,101},{38,102},{39,103... | collective-permute-start | bytes 110600 | tf_op jit(solution)/shard_map/ppermute | solution.py:330
  53.7 1.4 collective-permute-start.10
  54.3 0.7 collective-permute-start.11
  70.6 10.5 %collective-permute-start.13 = (bf16[64,1152]{1,0:T(8,128)(2,1)}, bf16[64,1152]{1,0:T(8,128)(2,1)S(1)}, u32[]{:S(2)}, u32[]{:S(2)}) collective-permute-start(bf16[64,1152]{1,0:T(8,128)(2,1)} %get-tuple-element.183), channel_id=1, source_target_pairs={{64,96},{65,97},{66,98},{67,99},{68,100},{69,101},{70,102},{71,103... | collective-permute-start | bytes 442376 | tf_op jit(solution)/shard_map/ppermute | solution.py:330
  71.9 9.2 %collective-permute-start.16 = (bf16[144,128]{1,0:T(8,128)(2,1)}, bf16[144,128]{1,0:T(8,128)(2,1)S(1)}, u32[]{:S(2)}, u32[]{:S(2)}) collective-permute-start(bf16[144,128]{1,0:T(8,128)(2,1)} %get-tuple-element.186), channel_id=1, source_target_pairs={{64,128},{65,129},{66,130},{67,131},{68,132},{69,133},{70,134},{71... | collective-permute-start | bytes 110600 | tf_op jit(solution)/shard_map/ppermute | solution.py:330
  72.5 6.4 %collective-permute-start.14 = (bf16[64,256]{1,0:T(8,128)(2,1)}, bf16[64,256]{1,0:T(8,128)(2,1)S(1)}, u32[]{:S(2)}, u32[]{:S(2)}) collective-permute-start(bf16[64,256]{1,0:T(8,128)(2,1)} %get-tuple-element.184), channel_id=1, source_target_pairs={{64,97},{65,98},{66,99},{67,100},{68,101},{69,102},{70,103},{71,10... | collective-permute-start | bytes 98312 | tf_op jit(solution)/shard_map/ppermute | solution.py:330
  73.8 7.3 %collective-permute-start.15 = (bf16[64,256]{1,0:T(8,128)(2,1)}, bf16[64,256]{1,0:T(8,128)(2,1)S(1)}, u32[]{:S(2)}, u32[]{:S(2)}) collective-permute-start(bf16[64,256]{1,0:T(8,128)(2,1)} %get-tuple-element.185), channel_id=1, source_target_pairs={{65,96},{66,97},{67,98},{68,99},{69,100},{70,101},{71,102},{72,103... | collective-permute-start | bytes 98312 | tf_op jit(solution)/shard_map/ppermute | solution.py:330
  82.8 2.8 collective-permute-start.17
  83.5 2.1 collective-permute-start.20
  84.2 1.4 collective-permute-start.18
  84.9 0.7 collective-permute-start.19
  87.4 13.6 %collective-permute-start.21 = (bf16[64,1152]{1,0:T(8,128)(2,1)}, bf16[64,1152]{1,0:T(8,128)(2,1)S(1)}, u32[]{:S(2)}, u32[]{:S(2)}) collective-permute-start(bf16[64,1152]{1,0:T(8,128)(2,1)} %get-tuple-element.195), channel_id=1, source_target_pairs={{32,64},{33,65},{34,66},{35,67},{36,68},{37,69},{38,70},{39,71},{4... | collective-permute-start | bytes 442376 | tf_op jit(solution)/shard_map/ppermute | solution.py:330
  88.1 12.9 %collective-permute-start.24 = (bf16[144,128]{1,0:T(8,128)(2,1)}, bf16[144,128]{1,0:T(8,128)(2,1)S(1)}, u32[]{:S(2)}, u32[]{:S(2)}) collective-permute-start(bf16[144,128]{1,0:T(8,128)(2,1)} %get-tuple-element.198), channel_id=1, source_target_pairs={{32,96},{33,97},{34,98},{35,99},{36,100},{37,101},{38,102},{39,103... | collective-permute-start | bytes 110600 | tf_op jit(solution)/shard_map/ppermute | solution.py:330
  89.4 1.4 collective-permute-start.22
  90.0 0.7 collective-permute-start.23
  102.8 13.1 %collective-permute-start.25 = (bf16[64,1152]{1,0:T(8,128)(2,1)}, bf16[64,1152]{1,0:T(8,128)(2,1)S(1)}, u32[]{:S(2)}, u32[]{:S(2)}) collective-permute-start(bf16[64,1152]{1,0:T(8,128)(2,1)} %get-tuple-element.201), channel_id=1, source_target_pairs={{64,96},{65,97},{66,98},{67,99},{68,100},{69,101},{70,102},{71,103... | collective-permute-start | bytes 442376 | tf_op jit(solution)/shard_map/ppermute | solution.py:330
  104.1 11.8 %collective-permute-start.28 = (bf16[144,128]{1,0:T(8,128)(2,1)}, bf16[144,128]{1,0:T(8,128)(2,1)S(1)}, u32[]{:S(2)}, u32[]{:S(2)}) collective-permute-start(bf16[144,128]{1,0:T(8,128)(2,1)} %get-tuple-element.204), channel_id=1, source_target_pairs={{64,128},{65,129},{66,130},{67,131},{68,132},{69,133},{70,134},{71... | collective-permute-start | bytes 110600 | tf_op jit(solution)/shard_map/ppermute | solution.py:330
  104.7 8.9 %collective-permute-start.26 = (bf16[64,256]{1,0:T(8,128)(2,1)}, bf16[64,256]{1,0:T(8,128)(2,1)S(1)}, u32[]{:S(2)}, u32[]{:S(2)}) collective-permute-start(bf16[64,256]{1,0:T(8,128)(2,1)} %get-tuple-element.202), channel_id=1, source_target_pairs={{64,97},{65,98},{66,99},{67,100},{68,101},{69,102},{70,103},{71,10... | collective-permute-start | bytes 98312 | tf_op jit(solution)/shard_map/ppermute | solution.py:330
  106.0 9.8 %collective-permute-start.27 = (bf16[64,256]{1,0:T(8,128)(2,1)}, bf16[64,256]{1,0:T(8,128)(2,1)S(1)}, u32[]{:S(2)}, u32[]{:S(2)}) collective-permute-start(bf16[64,256]{1,0:T(8,128)(2,1)} %get-tuple-element.203), channel_id=1, source_target_pairs={{65,96},{66,97},{67,98},{68,99},{69,100},{70,101},{71,102},{72,103... | collective-permute-start | bytes 98312 | tf_op jit(solution)/shard_map/ppermute | solution.py:330
  117.6 2.8 collective-permute-start.29
  118.3 2.1 collective-permute-start.32
  119.0 1.4 collective-permute-start.30
  119.7 0.7 collective-permute-start.31
  122.2 17.1 %collective-permute-start.33 = (bf16[64,1152]{1,0:T(8,128)(2,1)}, bf16[64,1152]{1,0:T(8,128)(2,1)S(1)}, u32[]{:S(2)}, u32[]{:S(2)}) collective-permute-start(bf16[64,1152]{1,0:T(8,128)(2,1)} %get-tuple-element.213), channel_id=1, source_target_pairs={{32,64},{33,65},{34,66},{35,67},{36,68},{37,69},{38,70},{39,71},{4... | collective-permute-start | bytes 442376 | tf_op jit(solution)/shard_map/ppermute | solution.py:330
  122.9 16.5 %collective-permute-start.36 = (bf16[144,128]{1,0:T(8,128)(2,1)}, bf16[144,128]{1,0:T(8,128)(2,1)S(1)}, u32[]{:S(2)}, u32[]{:S(2)}) collective-permute-start(bf16[144,128]{1,0:T(8,128)(2,1)} %get-tuple-element.216), channel_id=1, source_target_pairs={{32,96},{33,97},{34,98},{35,99},{36,100},{37,101},{38,102},{39,103... | collective-permute-start | bytes 110600 | tf_op jit(solution)/shard_map/ppermute | solution.py:330
  124.2 1.4 collective-permute-start.34
  124.8 0.7 collective-permute-start.35
  141.1 11.5 %collective-permute-start.37 = (bf16[64,1152]{1,0:T(8,128)(2,1)}, bf16[64,1152]{1,0:T(8,128)(2,1)S(1)}, u32[]{:S(2)}, u32[]{:S(2)}) collective-permute-start(bf16[64,1152]{1,0:T(8,128)(2,1)} %get-tuple-element.219), channel_id=1, source_target_pairs={{64,96},{65,97},{66,98},{67,99},{68,100},{69,101},{70,102},{71,103... | collective-permute-start | bytes 442376 | tf_op jit(solution)/shard_map/ppermute | solution.py:330
  142.4 10.2 %collective-permute-start.40 = (bf16[144,128]{1,0:T(8,128)(2,1)}, bf16[144,128]{1,0:T(8,128)(2,1)S(1)}, u32[]{:S(2)}, u32[]{:S(2)}) collective-permute-start(bf16[144,128]{1,0:T(8,128)(2,1)} %get-tuple-element.222), channel_id=1, source_target_pairs={{64,128},{65,129},{66,130},{67,131},{68,132},{69,133},{70,134},{71... | collective-permute-start | bytes 110600 | tf_op jit(solution)/shard_map/ppermute | solution.py:330
  143.0 7.7 %collective-permute-start.38 = (bf16[64,256]{1,0:T(8,128)(2,1)}, bf16[64,256]{1,0:T(8,128)(2,1)S(1)}, u32[]{:S(2)}, u32[]{:S(2)}) collective-permute-start(bf16[64,256]{1,0:T(8,128)(2,1)} %get-tuple-element.220), channel_id=1, source_target_pairs={{64,97},{65,98},{66,99},{67,100},{68,101},{69,102},{70,103},{71,10... | collective-permute-start | bytes 98312 | tf_op jit(solution)/shard_map/ppermute | solution.py:330
  144.3 8.2 %collective-permute-start.39 = (bf16[64,256]{1,0:T(8,128)(2,1)}, bf16[64,256]{1,0:T(8,128)(2,1)S(1)}, u32[]{:S(2)}, u32[]{:S(2)}) collective-permute-start(bf16[64,256]{1,0:T(8,128)(2,1)} %get-tuple-element.221), channel_id=1, source_target_pairs={{65,96},{66,97},{67,98},{68,99},{69,100},{70,101},{71,102},{72,103... | collective-permute-start | bytes 98312 | tf_op jit(solution)/shard_map/ppermute | solution.py:330
  154.3 2.8 collective-permute-start.41
  155.0 2.1 collective-permute-start.44
  155.7 1.4 collective-permute-start.42
  156.3 0.7 collective-permute-start.43
  158.9 15.5 %collective-permute-start.45 = (bf16[64,1152]{1,0:T(8,128)(2,1)}, bf16[64,1152]{1,0:T(8,128)(2,1)S(1)}, u32[]{:S(2)}, u32[]{:S(2)}) collective-permute-start(bf16[64,1152]{1,0:T(8,128)(2,1)} %get-tuple-element.231), channel_id=1, source_target_pairs={{32,64},{33,65},{34,66},{35,67},{36,68},{37,69},{38,70},{39,71},{4... | collective-permute-start | bytes 442376 | tf_op jit(solution)/shard_map/ppermute | solution.py:330
  159.5 14.8 %collective-permute-start.48 = (bf16[144,128]{1,0:T(8,128)(2,1)}, bf16[144,128]{1,0:T(8,128)(2,1)S(1)}, u32[]{:S(2)}, u32[]{:S(2)}) collective-permute-start(bf16[144,128]{1,0:T(8,128)(2,1)} %get-tuple-element.234), channel_id=1, source_target_pairs={{32,96},{33,97},{34,98},{35,99},{36,100},{37,101},{38,102},{39,103... | collective-permute-start | bytes 110600 | tf_op jit(solution)/shard_map/ppermute | solution.py:330
  160.8 1.4 collective-permute-start.46
  176.1 10.7 %collective-permute-start.49 = (bf16[64,1152]{1,0:T(8,128)(2,1)}, bf16[64,1152]{1,0:T(8,128)(2,1)S(1)}, u32[]{:S(2)}, u32[]{:S(2)}) collective-permute-start(bf16[64,1152]{1,0:T(8,128)(2,1)} %get-tuple-element.237), channel_id=1, source_target_pairs={{64,96},{65,97},{66,98},{67,99},{68,100},{69,101},{70,102},{71,103... | collective-permute-start | bytes 442376 | tf_op jit(solution)/shard_map/ppermute | solution.py:330
  177.4 9.4 %collective-permute-start.52 = (bf16[144,128]{1,0:T(8,128)(2,1)}, bf16[144,128]{1,0:T(8,128)(2,1)S(1)}, u32[]{:S(2)}, u32[]{:S(2)}) collective-permute-start(bf16[144,128]{1,0:T(8,128)(2,1)} %get-tuple-element.240), channel_id=1, source_target_pairs={{64,128},{65,129},{66,130},{67,131},{68,132},{69,133},{70,134},{71... | collective-permute-start | bytes 110600 | tf_op jit(solution)/shard_map/ppermute | solution.py:330
  178.0 7.2 %collective-permute-start.50 = (bf16[64,256]{1,0:T(8,128)(2,1)}, bf16[64,256]{1,0:T(8,128)(2,1)S(1)}, u32[]{:S(2)}, u32[]{:S(2)}) collective-permute-start(bf16[64,256]{1,0:T(8,128)(2,1)} %get-tuple-element.238), channel_id=1, source_target_pairs={{64,97},{65,98},{66,99},{67,100},{68,101},{69,102},{70,103},{71,10... | collective-permute-start | bytes 98312 | tf_op jit(solution)/shard_map/ppermute | solution.py:330
  179.3 7.4 %collective-permute-start.51 = (bf16[64,256]{1,0:T(8,128)(2,1)}, bf16[64,256]{1,0:T(8,128)(2,1)S(1)}, u32[]{:S(2)}, u32[]{:S(2)}) collective-permute-start(bf16[64,256]{1,0:T(8,128)(2,1)} %get-tuple-element.239), channel_id=1, source_target_pairs={{65,96},{66,97},{67,98},{68,99},{69,100},{70,101},{71,102},{72,103... | collective-permute-start | bytes 98312 | tf_op jit(solution)/shard_map/ppermute | solution.py:330
  188.5 3.0 collective-permute-start.53
  189.2 2.3 collective-permute-start.56
  189.8 1.6 collective-permute-start.54
  190.5 1.0 collective-permute-start.55
  193.3 72.4 %collective-permute-start.57 = (bf16[64,1152]{1,0:T(8,128)(2,1)}, bf16[64,1152]{1,0:T(8,128)(2,1)S(1)}, u32[]{:S(2)}, u32[]{:S(2)}) collective-permute-start(bf16[64,1152]{1,0:T(8,128)(2,1)} %get-tuple-element.249), channel_id=1, source_target_pairs={{32,64},{33,65},{34,66},{35,67},{36,68},{37,69},{38,70},{39,71},{4... | collective-permute-start | bytes 442376 | tf_op jit(solution)/shard_map/ppermute | solution.py:330
  193.9 71.7 %collective-permute-start.60 = (bf16[144,128]{1,0:T(8,128)(2,1)}, bf16[144,128]{1,0:T(8,128)(2,1)S(1)}, u32[]{:S(2)}, u32[]{:S(2)}) collective-permute-start(bf16[144,128]{1,0:T(8,128)(2,1)} %get-tuple-element.252), channel_id=1, source_target_pairs={{32,96},{33,97},{34,98},{35,99},{36,100},{37,101},{38,102},{39,103... | collective-permute-start | bytes 110600 | tf_op jit(solution)/shard_map/ppermute | solution.py:330
  195.2 1.4 collective-permute-start.58
  267.4 17.8 %collective-permute-start.61 = (bf16[64,1152]{1,0:T(8,128)(2,1)}, bf16[64,1152]{1,0:T(8,128)(2,1)S(1)}, u32[]{:S(2)}, u32[]{:S(2)}) collective-permute-start(bf16[64,1152]{1,0:T(8,128)(2,1)} %get-tuple-element.255), channel_id=1, source_target_pairs={{64,96},{65,97},{66,98},{67,99},{68,100},{69,101},{70,102},{71,103... | collective-permute-start | bytes 442376 | tf_op jit(solution)/shard_map/ppermute | solution.py:330
  268.7 16.5 %collective-permute-start.64 = (bf16[144,128]{1,0:T(8,128)(2,1)}, bf16[144,128]{1,0:T(8,128)(2,1)S(1)}, u32[]{:S(2)}, u32[]{:S(2)}) collective-permute-start(bf16[144,128]{1,0:T(8,128)(2,1)} %get-tuple-element.258), channel_id=1, source_target_pairs={{64,96},{65,97},{66,98},{67,99},{68,100},{69,101},{70,102},{71,103... | collective-permute-start | bytes 110600 | tf_op jit(solution)/shard_map/ppermute | solution.py:330
  270.0 15.2 %collective-permute-start.62 = (bf16[64,256]{1,0:T(8,128)(2,1)}, bf16[64,256]{1,0:T(8,128)(2,1)S(1)}, u32[]{:S(2)}, u32[]{:S(2)}) collective-permute-start(bf16[64,256]{1,0:T(8,128)(2,1)} %get-tuple-element.256), channel_id=1, source_target_pairs={{64,97},{65,98},{66,99},{67,100},{68,101},{69,102},{70,103},{71,10... | collective-permute-start | bytes 98312 | tf_op jit(solution)/shard_map/ppermute | solution.py:330
  271.3 13.9 %collective-permute-start.63 = (bf16[64,256]{1,0:T(8,128)(2,1)}, bf16[64,256]{1,0:T(8,128)(2,1)S(1)}, u32[]{:S(2)}, u32[]{:S(2)}) collective-permute-start(bf16[64,256]{1,0:T(8,128)(2,1)} %get-tuple-element.257), channel_id=1, source_target_pairs={{65,96},{66,97},{67,98},{68,99},{69,100},{70,101},{71,102},{72,103... | collective-permute-start | bytes 98312 | tf_op jit(solution)/shard_map/ppermute | solution.py:330
  291.6 12.9 %collective-permute-start.65 = (bf16[32,256]{1,0:T(8,128)(2,1)}, bf16[32,256]{1,0:T(8,128)(2,1)S(1)}, u32[]{:S(2)}, u32[]{:S(2)}) collective-permute-start(bf16[32,256]{1,0:T(8,128)(2,1)} %get-tuple-element.261), channel_id=1, source_target_pairs={{32,0},{64,32},{96,64},{128,96},{160,128},{192,160},{224,192},{256... | collective-permute-start | bytes 49160 | tf_op jit(solution)/shard_map/ppermute | solution.py:320
  (55 other events, 286.9 us)
